TPU v7x, 32 devices: a whole 2x2x4 slice. The times are simulated.
32 devices in a mesh: rep: 4 (over z), member: 8 (over y, x, core).
Axes of the slice: x: 2, y: 2, z: 4, core: 2. Of those that a mesh axis runs over, the one named last changes fastest.
Arguments:
- acts: bfloat16 [512, 2, 100, 128], P(('rep', 'member')), may hold values from -6 to 6
- cotangent: bfloat16 [512, 2, 100, 128], P(('rep', 'member')), may hold values from -6 to 6
- routes: int32 [512, 2], P(('rep', 'member')), may hold values from 0 to 7, all different within a row; in each aligned block of 16 rows (0 to 15, 16 to 31, ...) at most 8 rows name the same one
- w_first: bfloat16 [8, 1152, 128], P('member'), may hold values from -0.1875 to 0.1875
- w_second: bfloat16 [8, 1152, 128], P('member'), may hold values from -0.1875 to 0.1875
- b_first: float32 [8, 128], P('member'), may hold values from -3 to 3
- b_second: float32 [8, 128], P('member'), may hold values from -3 to 3
Outputs:
- out_acts: bfloat16 [512, 2, 100, 128], P(('rep', 'member'))
- grad_acts: bfloat16 [512, 2, 100, 128], P(('rep', 'member'))
- grad_w_first: float32 [8, 1152, 128], P('member')
- grad_w_second: float32 [8, 1152, 128], P('member')
- grad_b_first: float32 [8, 128], P('member')
- grad_b_second: float32 [8, 128], P('member')
Inputs may be any that keep to these rules, and one draw needn't show every extreme that they name: `routes`: the two members of a state differ. Among the 16 states of one device no member is named more than 8 times, and in some device one member is named exactly 8 times. Every member is named by some state.
All inputs are finite; a program needn't handle non-finite values.
Results may differ from a plain program's by a relative error of at most 0.007.
Values may be sent and summed in bfloat16 or wider, within the bound.
A program may use at most 64 MiB of HBM per device.

v0:
```python
import jax
import jax.numpy as jnp
from jax import lax
from jax.sharding import PartitionSpec as P

BOARD = 10


def flipped(weight):
    channels = weight.shape[-1]
    stacked = weight.reshape(weight.shape[:-2] + (9, channels, channels))
    reversed_taps = jnp.flip(stacked, axis=-3)
    return jnp.swapaxes(reversed_taps, -1, -2).reshape(weight.shape)


def silu_slope(pre_act):
    sigmoid_vals = jax.nn.sigmoid(pre_act)
    return sigmoid_vals * (1.0 + pre_act * (1.0 - sigmoid_vals))


def board_conv(values, weight):
    count = values.shape[0]
    channels = values.shape[-1]
    side = BOARD
    boards = values.reshape(count, side, side, channels)
    kernel = weight.reshape(3, 3, channels, channels)
    result = lax.conv_general_dilated(
        boards,
        kernel,
        (1, 1),
        ((1, 1), (1, 1)),
        dimension_numbers=("NHWC", "HWIO", "NHWC"),
        preferred_element_type=jnp.float32,
    )
    return result.reshape(count, side * side, channels)


def weight_conv(values, grads):
    count = values.shape[0]
    channels = values.shape[-1]
    side = BOARD
    boards = values.reshape(count, side, side, channels)
    grad_boards = grads.reshape(count, side, side, channels)
    result = lax.conv_general_dilated(
        boards,
        grad_boards,
        (1, 1),
        ((1, 1), (1, 1)),
        dimension_numbers=("CHWN", "IHWO", "NHWC"),
        preferred_element_type=jnp.float32,
    )
    return jnp.transpose(result, (1, 2, 0, 3)).reshape(9 * channels, channels)


def shards(acts, cotangent, routes, w_first, w_second, b_first, b_second):
    per_owner = w_first.shape[0]
    owners = lax.axis_size("member")
    members_all = owners * per_owner
    capacity = max(2, 4 * routes.shape[0] // members_all)
    channels = acts.shape[-1]
    cell_count = acts.shape[-2]
    member_ids = routes.reshape(-1)
    onehot = (member_ids[:, None] == jnp.arange(members_all, dtype=jnp.int32)[None, :]).astype(
        jnp.int32
    )
    earlier = jnp.cumsum(onehot, axis=0) - onehot
    slot_index = jnp.sum(earlier * onehot, axis=1)
    target = member_ids * capacity + slot_index
    dispatch = (
        jnp.arange(members_all * capacity, dtype=jnp.int32)[:, None] == target[None, :]
    ).astype(jnp.bfloat16)

    def scatter_rows(values):
        flattened = values.reshape(-1, cell_count * channels)
        placed = jnp.dot(dispatch, flattened, preferred_element_type=jnp.float32).astype(
            jnp.bfloat16
        )
        return placed.reshape(members_all, capacity, cell_count, channels)

    def gather_rows(values):
        flattened = values.reshape(members_all * capacity, cell_count * channels)
        picked = jnp.dot(dispatch.T, flattened, preferred_element_type=jnp.float32).astype(
            jnp.bfloat16
        )
        return picked.reshape(acts.shape)

    def to_local(received):
        grouped = received.reshape(owners, per_owner, capacity, cell_count, channels)
        return jnp.swapaxes(grouped, 0, 1).reshape(
            per_owner, owners * capacity, cell_count, channels
        )

    def from_local(values):
        grouped = values.reshape(per_owner, owners, capacity, cell_count, channels)
        return jnp.swapaxes(grouped, 0, 1).reshape(members_all, capacity, cell_count, channels)

    send_acts = scatter_rows(acts)
    send_grads = scatter_rows(cotangent)
    recv_acts, recv_grads = (
        lax.all_to_all(send_acts, "member", split_axis=0, concat_axis=0, tiled=True),
        lax.all_to_all(send_grads, "member", split_axis=0, concat_axis=0, tiled=True),
    )
    inputs = to_local(recv_acts)
    upstream = to_local(recv_grads)
    owned = 0
    pre_one = board_conv(inputs[owned], w_first[owned]) + b_first[owned][None, None, :]
    hidden_one = jax.nn.silu(pre_one).astype(jnp.bfloat16)
    result_one = (
        inputs[owned].astype(jnp.float32)
        + board_conv(hidden_one, w_second[owned])
        + b_second[owned][None, None, :]
    ).astype(jnp.bfloat16)
    pre_list = [pre_one]
    hidden_list = [hidden_one]
    result_list = [result_one]
    result = jnp.stack(result_list)
    owned = 0
    upstream_one = upstream[owned]
    grad_two_list = [weight_conv(hidden_list[owned], upstream_one)]
    bias_two_list = [jnp.sum(upstream_one.astype(jnp.float32), axis=(0, 1))]
    hidden_grad = board_conv(upstream_one, flipped(w_second[owned]))
    pre_grad = (hidden_grad * silu_slope(pre_list[owned])).astype(jnp.bfloat16)
    grad_one_list = [weight_conv(inputs[owned], pre_grad)]
    bias_one_list = [jnp.sum(pre_grad.astype(jnp.float32), axis=(0, 1))]
    input_list = [
        (upstream_one.astype(jnp.float32) + board_conv(pre_grad, flipped(w_first[owned]))).astype(
            jnp.bfloat16
        )
    ]
    input_grad = jnp.stack(input_list)
    grad_one = jnp.stack(grad_one_list)
    grad_two = jnp.stack(grad_two_list)
    bias_one = jnp.stack(bias_one_list)
    bias_two = jnp.stack(bias_two_list)
    back_out, back_in = (
        lax.all_to_all(from_local(result), "member", split_axis=0, concat_axis=0, tiled=True),
        lax.all_to_all(from_local(input_grad), "member", split_axis=0, concat_axis=0, tiled=True),
    )
    totals = lax.psum((grad_one, grad_two, bias_one, bias_two), "rep")
    return (gather_rows(back_out), gather_rows(back_in), totals[0], totals[1], totals[2], totals[3])


def solution(mesh):
    placed = (
        P(("rep", "member"), None, None, None),
        P(("rep", "member"), None, None, None),
        P(("rep", "member"), None),
        P("member", None, None),
        P("member", None, None),
        P("member", None),
        P("member", None),
    )
    return jax.shard_map(
        shards,
        mesh=mesh,
        in_specs=placed,
        out_specs=(
            P(("rep", "member"), None, None, None),
            P(("rep", "member"), None, None, None),
            P("member", None, None),
            P("member", None, None),
            P("member", None),
            P("member", None),
        ),
        check_vma=False,
    )
```

profile of v0, /device:TPU:0, one launch (start us, length us, event | category | flops | bytes accessed | tf_op | source)
XLA Modules:
  0.0 168.1 jit_solution(13357833731304342568)
XLA Ops:
  7.2 0.8 copy.22
  7.9 0.1 reshape.64
  8.0 0.1 fusion.15
  8.1 0.1 reduce_window_sum.11
  8.1 0.2 select_reduce_fusion
  8.3 1.3 copy.23
  9.6 1.8 %fusion.5 = bf16[8,8,100,128]{3,1,2,0:T(8,128)(2,1)} fusion(bf16[4,8,100,128]{3,2,1,0:T(8,128)(2,1)S(1)} %bitcast.55, s32[32]{0:T(128)S(1)} %multiply_add_fusion), kind=kOutput, calls=%fused_computation.16 | convolution fusion | flops 53250048 | bytes 2457728 | tf_op jit(solution)/shard_map/dot_general | solution.py:75
  11.4 5.3 %all-to-all-start = ((bf16[8,8,100,128]{3,1,2,0:T(8,128)(2,1)}), bf16[8,8,100,128]{3,1,2,0:T(8,128)(2,1)S(1)}, u32[]{:S(2)}, u32[]{:S(2)}) async-start(bf16[8,8,100,128]{3,1,2,0:T(8,128)(2,1)} %fusion.5), calls=%async_computation | async-start | bytes 3276800 | tf_op jit(solution)/shard_map/all_to_all | solution.py:100
  16.7 0.0 copy-done.4
  16.7 0.1 copy.26
  16.8 1.8 %fusion.6 = bf16[8,8,100,128]{3,1,2,0:T(8,128)(2,1)} fusion(bf16[4,8,100,128]{3,2,1,0:T(8,128)(2,1)S(1)} %bitcast.56, s32[32]{0:T(128)S(1)} %multiply_add_fusion), kind=kOutput, calls=%fused_computation.17 | convolution fusion | flops 53250048 | bytes 2457728 | tf_op jit(solution)/shard_map/dot_general | solution.py:75
  18.6 19.8 %all-to-all-done = bf16[8,8,100,128]{3,1,2,0:T(8,128)(2,1)S(1)} async-done(((bf16[8,8,100,128]{3,1,2,0:T(8,128)(2,1)}), bf16[8,8,100,128]{3,1,2,0:T(8,128)(2,1)S(1)}, u32[]{:S(2)}, u32[]{:S(2)}) %all-to-all-start) | async-done | bytes 1638432 | tf_op jit(solution)/shard_map/all_to_all | solution.py:100
  38.4 3.6 %all-to-all-start.2 = ((bf16[8,8,100,128]{3,1,2,0:T(8,128)(2,1)}), bf16[8,8,100,128]{3,1,2,0:T(8,128)(2,1)S(1)}, u32[]{:S(2)}, u32[]{:S(2)}) async-start(bf16[8,8,100,128]{3,1,2,0:T(8,128)(2,1)} %fusion.6), calls=%async_computation.2 | async-start | bytes 3276800 | tf_op jit(solution)/shard_map/all_to_all | solution.py:101
  42.0 1.7 %rev.7 = bf16[9,128,128]{2,1,0:T(8,128)(2,1)} reverse(bf16[9,128,128]{2,1,0:T(8,128)(2,1)} %bitcast.62), dimensions={0} | reverse | bytes 589824 | tf_op jit(solution)/shard_map/jit(_flip)/rev | solution.py:12
  43.7 1.7 %rev.8 = bf16[9,128,128]{2,1,0:T(8,128)(2,1)} reverse(bf16[9,128,128]{2,1,0:T(8,128)(2,1)} %bitcast.66), dimensions={0} | reverse | bytes 589824 | tf_op jit(solution)/shard_map/jit(_flip)/rev | solution.py:12
  45.4 0.5 copy.24
  45.9 0.0 copy-start.2
  45.9 0.5 copy-done.5
  46.3 5.9 %multiply_convert_fusion.1 = (bf16[64,10,10,128]{3,0,2,1:T(8,128)(2,1)S(1)}, f32[64,10,10,128]{3,0,2,1:T(8,128)}) fusion(f32[128]{0:T(128)S(1)} %bitcast.72, bf16[64,10,10,128]{3,0,2,1:T(8,128)(2,1)S(1)} %bitcast.58, bf16[3,3,128,128]{3,2,1,0:T(8,128)(2,1)S(1)} %bitcast.67), kind=kOutput, calls=%fused_computation.12 | convolution fusion | flops 1649082368 | bytes 6849024 | tf_op jit(solution)/shard_map/conv_general_dilated | solution.py:27
  52.3 4.1 %fusion.16 = f32[64,10,10,128]{3,0,2,1:T(8,128)S(1)} fusion(bf16[64,10,10,128]{3,0,2,1:T(8,128)(2,1)S(1)} %get-tuple-element.24, bf16[3,3,128,128]{3,2,1,0:T(8,128)(2,1)S(1)} %bitcast.63), kind=kOutput, calls=%fused_computation.31 | convolution fusion | flops 1644167168 | bytes 5210112 | tf_op jit(solution)/shard_map/conv_general_dilated | solution.py:27
  56.4 0.0 copy-done
  56.4 0.0 copy-done.8
  56.5 1.7 fusion.2
  58.1 5.5 %all-to-all-done.2 = bf16[8,8,100,128]{3,1,2,0:T(8,128)(2,1)S(1)} async-done(((bf16[8,8,100,128]{3,1,2,0:T(8,128)(2,1)}), bf16[8,8,100,128]{3,1,2,0:T(8,128)(2,1)S(1)}, u32[]{:S(2)}, u32[]{:S(2)}) %all-to-all-start.2) | async-done | bytes 1638432 | tf_op jit(solution)/shard_map/all_to_all | solution.py:101
  63.7 3.8 %all-to-all-start.1 = ((bf16[8,8,100,128]{3,1,2,0:T(8,128)(2,1)}), bf16[8,8,100,128]{3,1,2,0:T(8,128)(2,1)S(1)}, u32[]{:S(2)}, u32[]{:S(2)}) async-start(bf16[8,8,100,128]{3,1,2,0:T(8,128)(2,1)} %fusion.2), calls=%async_computation.1 | async-start | bytes 3276800 | tf_op jit(solution)/shard_map/all_to_all | solution.py:136
  67.4 0.0 copy-start.7
  67.4 0.5 copy.27
  67.9 0.5 copy-done.7
  68.4 6.2 %convert_reduce_fusion.1 = (f32[128]{0:T(128)S(1)}, bf16[64,10,10,128]{3,0,2,1:T(8,128)(2,1)S(1)}) fusion(f32[64,10,10,128]{3,0,2,1:T(8,128)} %get-tuple-element.25, f32[128]{0:T(128)S(1)} %bitcast.73, bf16[64,10,10,128]{3,0,2,1:T(8,128)(2,1)S(1)} %bitcast.60, bf16[3,3,128,128]{2,3,1,0:T(8,128)(2,1)S(1)} %bitcast.69), kind=kOutput, calls=%fused_computation.10 | convolution fusion | flops 1653997440 | bytes 6849536 | tf_op jit(solution)/shard_map/conv_general_dilated | solution.py:27
  74.7 4.1 %fusion.17 = f32[64,10,10,128]{3,0,2,1:T(8,128)S(1)} fusion(bf16[64,10,10,128]{3,0,2,1:T(8,128)(2,1)S(1)} %get-tuple-element.27, bf16[3,3,128,128]{2,3,1,0:T(8,128)(2,1)S(1)} %bitcast.68), kind=kOutput, calls=%fused_computation.32 | convolution fusion | flops 1644167168 | bytes 5210112 | tf_op jit(solution)/shard_map/conv_general_dilated | solution.py:27
  78.8 2.0 %convert_reduce_fusion = (f32[128]{0:T(128)S(1)}, bf16[8,8,100,128]{3,1,2,0:T(8,128)(2,1)}) fusion(bf16[8,8,100,128]{3,1,2,0:T(8,128)(2,1)S(1)} %all-to-all-done.2, f32[8,8,100,128]{3,1,0,2:T(8,128)S(1)} %bitcast.57), kind=kLoop, calls=%fused_computation.4 | loop fusion | flops 3276672 | bytes 6554112 | tf_op jit(solution)/shard_map/reduce_sum | solution.py:120
  80.8 4.9 %fusion.19 = f32[3,3,128,128]{3,2,1,0:T(8,128)} fusion(bf16[64,10,10,128]{3,0,2,1:T(8,128)(2,1)S(1)} %copy-done.1, bf16[64,10,10,128]{3,0,2,1:T(8,128)(2,1)S(1)} %bitcast.61), kind=kOutput, calls=%fused_computation.34 | convolution fusion | flops 1644167168 | bytes 3866624 | tf_op jit(solution)/shard_map/transpose | solution.py:52
  85.6 3.3 %all-to-all-done.1 = bf16[8,8,100,128]{3,1,2,0:T(8,128)(2,1)S(1)} async-done(((bf16[8,8,100,128]{3,1,2,0:T(8,128)(2,1)}), bf16[8,8,100,128]{3,1,2,0:T(8,128)(2,1)S(1)}, u32[]{:S(2)}, u32[]{:S(2)}) %all-to-all-start.1) | async-done | bytes 1638432 | tf_op jit(solution)/shard_map/all_to_all | solution.py:136
  88.9 3.6 %all-to-all-start.3 = ((bf16[8,8,100,128]{3,1,2,0:T(8,128)(2,1)}), bf16[8,8,100,128]{3,1,2,0:T(8,128)(2,1)S(1)}, u32[]{:S(2)}, u32[]{:S(2)}) async-start(bf16[8,8,100,128]{3,1,2,0:T(8,128)(2,1)} %get-tuple-element.23), calls=%async_computation.3 | async-start | bytes 3276800 | tf_op jit(solution)/shard_map/all_to_all | solution.py:137
  92.5 0.3 all-reduce.4.cloned.1.call-start
  92.8 6.8 %fusion.18 = f32[3,3,128,128]{3,2,1,0:T(8,128)} fusion(bf16[64,10,10,128]{3,0,2,1:T(8,128)(2,1)} %bitcast.59, bf16[64,10,10,128]{3,0,2,1:T(8,128)(2,1)} %copy-done.10), kind=kOutput, calls=%fused_computation.33 | convolution fusion | flops 1644167168 | bytes 3866624 | tf_op jit(solution)/shard_map/transpose | solution.py:52
  99.5 0.0 all-reduce.4.cloned.1.call-update
  99.6 12.5 %all-reduce = (f32[1,128]{1,0:T(1,128)}, f32[1,128]{1,0:T(1,128)}) all-reduce(f32[1,128]{1,0:T(1,128)S(1)} %bitcast.74, f32[1,128]{1,0:T(1,128)S(1)} %bitcast.71), channel_id=1, replica_groups=mesh['rep'=4,'member'=8] {'rep'}, use_global_device_ids=true, to_apply=%region_5.6 | all-reduce | flops 256 | bytes 2048 | tf_op jit(solution)/shard_map/psum | solution.py:139
  112.1 1.3 convolution_convert_fusion.3
  113.4 1.6 reshape.69
  114.9 1.5 copy.31
  116.5 0.0 all-to-all-done.3
  116.5 1.3 convolution_convert_fusion.2
  117.8 1.5 reshape.74
  119.3 1.5 copy.32
  120.9 36.6 %all-reduce.4.cloned.1.call-done = (f32[1,1152,128]{2,1,0:T(8,128)}, f32[1,1152,128]{2,1,0:T(8,128)}) async-done(((f32[1,1152,128]{2,1,0:T(8,128)}, f32[1,1152,128]{2,1,0:T(8,128)}), (f32[1,1152,128]{2,1,0:T(8,128)}, f32[1,1152,128]{2,1,0:T(8,128)})) %all-reduce.4.cloned.1.call-update) | async-done | bytes 1179664 | tf_op jit(solution)/shard_map/psum | solution.py:139
  157.4 1.9 %copy.51 = f32[1,1152,128]{2,1,0:T(8,128)} copy(f32[1,1152,128]{2,1,0:T(8,128)} %get-tuple-element.30) | data formatting | bytes 1179648
  159.3 1.9 %copy.52 = f32[1,1152,128]{2,1,0:T(8,128)} copy(f32[1,1152,128]{2,1,0:T(8,128)} %get-tuple-element.31) | data formatting | bytes 1179648
  (16 shorter events, 0.0 us)
Async XLA Ops:
  11.4 5.3 %copy-start.4 = (bf16[16,2,100,128]{3,1,2,0:T(2,128)(2,1)S(1)}, bf16[16,2,100,128]{3,1,2,0:T(2,128)(2,1)}, u32[]{:S(2)}) copy-start(bf16[16,2,100,128]{3,1,2,0:T(2,128)(2,1)} %param.8) | copy-start | bytes 2457604
  11.4 27.0 %all-to-all-start = ((bf16[8,8,100,128]{3,1,2,0:T(8,128)(2,1)}), bf16[8,8,100,128]{3,1,2,0:T(8,128)(2,1)S(1)}, u32[]{:S(2)}, u32[]{:S(2)}) async-start(bf16[8,8,100,128]{3,1,2,0:T(8,128)(2,1)} %fusion.5), calls=%async_computation | async-start | bytes 3276800 | tf_op jit(solution)/shard_map/all_to_all | solution.py:100
  38.4 25.3 %all-to-all-start.2 = ((bf16[8,8,100,128]{3,1,2,0:T(8,128)(2,1)}), bf16[8,8,100,128]{3,1,2,0:T(8,128)(2,1)S(1)}, u32[]{:S(2)}, u32[]{:S(2)}) async-start(bf16[8,8,100,128]{3,1,2,0:T(8,128)(2,1)} %fusion.6), calls=%async_computation.2 | async-start | bytes 3276800 | tf_op jit(solution)/shard_map/all_to_all | solution.py:101
  45.4 1.0 copy-start.5
  45.4 1.0 copy-start.9
  45.9 6.4 %copy-start.2 = (bf16[8,8,100,128]{3,1,0,2:T(8,128)(2,1)}, bf16[8,8,100,128]{3,1,0,2:T(8,128)(2,1)S(1)}, u32[]{:S(2)}) copy-start(bf16[8,8,100,128]{3,1,0,2:T(8,128)(2,1)S(1)} %copy.24) | copy-start | bytes 4915204
  46.3 5.9 %copy-start.3 = (bf16[1,1152,128]{2,1,0:T(8,128)(2,1)S(1)}, bf16[1,1152,128]{2,1,0:T(8,128)(2,1)}, u32[]{:S(2)}) copy-start(bf16[1,1152,128]{2,1,0:T(8,128)(2,1)} %param.11) | copy-start | bytes 884740
  52.3 4.2 %copy-start = (bf16[64,10,10,128]{3,0,2,1:T(8,128)(2,1)}, bf16[64,10,10,128]{3,0,2,1:T(8,128)(2,1)S(1)}, u32[]{:S(2)}) copy-start(bf16[64,10,10,128]{3,0,2,1:T(8,128)(2,1)S(1)} %get-tuple-element.24) | copy-start | bytes 4915204
  52.3 4.2 %copy-start.8 = (f32[1,128]{1,0:T(1,128)S(1)}, f32[1,128]{1,0:T(1,128)}, u32[]{:S(2)}) copy-start(f32[1,128]{1,0:T(1,128)} %param.13) | copy-start | bytes 1540
  63.7 25.3 %all-to-all-start.1 = ((bf16[8,8,100,128]{3,1,2,0:T(8,128)(2,1)}), bf16[8,8,100,128]{3,1,2,0:T(8,128)(2,1)S(1)}, u32[]{:S(2)}, u32[]{:S(2)}) async-start(bf16[8,8,100,128]{3,1,2,0:T(8,128)(2,1)} %fusion.2), calls=%async_computation.1 | async-start | bytes 3276800 | tf_op jit(solution)/shard_map/all_to_all | solution.py:136
  67.4 1.0 copy-start.7
  68.4 6.3 %copy-start.6 = (bf16[9,128,128]{2,1,0:T(8,128)(2,1)S(1)}, bf16[9,128,128]{2,1,0:T(8,128)(2,1)}, u32[]{:S(2)}) copy-start(bf16[9,128,128]{2,1,0:T(8,128)(2,1)} %rev.8) | copy-start | bytes 884740
  74.6 4.1 %copy-start.10 = (bf16[64,10,10,128]{3,0,2,1:T(8,128)(2,1)}, bf16[64,10,10,128]{3,0,2,1:T(8,128)(2,1)S(1)}, u32[]{:S(2)}) copy-start(bf16[64,10,10,128]{3,0,2,1:T(8,128)(2,1)S(1)} %get-tuple-element.27) | copy-start | bytes 4915204
  78.8 2.0 %copy-start.1 = (bf16[64,10,10,128]{3,0,2,1:T(8,128)(2,1)S(1)}, bf16[64,10,10,128]{3,0,2,1:T(8,128)(2,1)}, u32[]{:S(2)}) copy-start(bf16[64,10,10,128]{3,0,2,1:T(8,128)(2,1)} %copy-done) | copy-start | bytes 4915204
  88.9 27.6 %all-to-all-start.3 = ((bf16[8,8,100,128]{3,1,2,0:T(8,128)(2,1)}), bf16[8,8,100,128]{3,1,2,0:T(8,128)(2,1)S(1)}, u32[]{:S(2)}, u32[]{:S(2)}) async-start(bf16[8,8,100,128]{3,1,2,0:T(8,128)(2,1)} %get-tuple-element.23), calls=%async_computation.3 | async-start | bytes 3276800 | tf_op jit(solution)/shard_map/all_to_all | solution.py:137
  92.5 64.9 %all-reduce.4.cloned.1.call-start = ((), (), s32[]{:S(2)}) async-start(), calls=%async_computation.4 | async-start | bytes 2359296 | tf_op jit(solution)/shard_map/psum | solution.py:139
Sparse Core Ops, SparseCore 0:
  99.7 57.6 all-reduce.3
where the time goes:
time: 169 us; the launch traced here: 168 us
  waiting for transfers between devices  65.2 us (39%)
  matrix products  38.2 us (23%)
  local copies, waits for them, and re-layouts  17.5 us (10%)
  starting transfers between devices  16.5 us (10%)
  between operations  14.2 us (8%)
  blocking collectives  12.5 us (7%)
  other arithmetic  3.95 us (2%)
    psum x1, waiting for transfers between devices, shards(): totals = lax.psum((grad_one, grad_two, bias_one, bias_two), 'rep')  36.6 us
    conv_general_dilated x4, matrix products, board_conv(): lax.conv_general_dilated(boards, kernel, (1, 1), ((1, 1), (1, 1)), dimens...  20.4 us
    all_to_all x1, waiting for transfers between devices, shards(): lax.all_to_all(send_acts, 'member', split_axis=0, concat_axis=0, tiled=True)  19.8 us
    psum x1, blocking collectives, shards(): totals = lax.psum((grad_one, grad_two, bias_one, bias_two), 'rep')  12.5 us
    transpose x2, matrix products, weight_conv(): return jnp.transpose(result, (1, 2, 0, 3)).reshape(9 * channels, channels)  11.6 us
    unnamed x29, local copies, waits for them, and re-layouts  10 us
    all_to_all x1, waiting for transfers between devices, shards(): lax.all_to_all(send_grads, 'member', split_axis=0, concat_axis=0, tiled=T...  5.54 us
    all_to_all x1, starting transfers between devices, shards(): lax.all_to_all(send_acts, 'member', split_axis=0, concat_axis=0, tiled=True)  5.3 us
  transfers between devices with their start and end apart: 5, of which 4 were waited for; matrix products, arithmetic and copies ran while one was open for 30% of the time, Pallas kernels for 0%

commit v1 on v0

--- a/solution.py
+++ b/solution.py
@@ -1,6 +1,10 @@
+import functools
+
 import jax
 import jax.numpy as jnp
 from jax import lax
+from jax.experimental import pallas as pl
+from jax.experimental.pallas import tpu as pltpu
 from jax.sharding import PartitionSpec as P
 
 BOARD = 10
@@ -63,7 +67,8 @@
     onehot = (member_ids[:, None] == jnp.arange(members_all, dtype=jnp.int32)[None, :]).astype(
         jnp.int32
     )
-    earlier = jnp.cumsum(onehot, axis=0) - onehot
+    order = jnp.arange(member_ids.shape[0], dtype=jnp.int32)
+    earlier = jnp.sum((order[:, None] > order[None, :])[:, :, None] * onehot[None], axis=1)
     slot_index = jnp.sum(earlier * onehot, axis=1)
     target = member_ids * capacity + slot_index
     dispatch = (
@@ -140,6 +145,279 @@
     return (gather_rows(back_out), gather_rows(back_in), totals[0], totals[1], totals[2], totals[3])
 
 
+SLOTS = 8
+SIDE = BOARD + 2
+CELLS = BOARD * BOARD
+ROWS = CELLS * SLOTS
+LINE = BOARD * SLOTS
+TAIL = 64
+
+
+def inner(line):
+    return ((line + 1) * SIDE + 1) * SLOTS
+
+
+def fill_patches(board_ref, patch_ref, channels):
+    for tap in range(9):
+        down, right = tap // 3, tap % 3
+        for line in range(BOARD):
+            start = ((line + down) * SIDE + right) * SLOTS
+            patch_ref[line * LINE : (line + 1) * LINE, tap * channels : (tap + 1) * channels] = (
+                board_ref[start : start + LINE, :].astype(jnp.bfloat16)
+            )
+
+
+def flipped_wide(weight_ref, base, channels):
+    return jnp.concatenate(
+        [
+            weight_ref[base + (8 - tap) * channels : base + (9 - tap) * channels, :]
+            for tap in range(9)
+        ],
+        axis=1,
+    )
+
+
+def tower_kernel(extra, slots_ref, acts_ref, cot_ref, weight_ref, *rest):
+    rest = rest[extra:]
+    (out_ref, back_ref, grads_ref, xs, gs, hs, ps, px, ph, pq, slope, flat_out, flat_back, stage, sems) = rest
+    channels = weight_ref.shape[-1]
+    taps = 9 * channels
+    f32, bf16 = jnp.float32, jnp.bfloat16
+    count = slots_ref[SLOTS]
+    for ref in (xs, gs, hs, ps):
+        ref[...] = jnp.zeros_like(ref)
+    for slot in range(SLOTS):
+
+        @pl.when(slot < count)
+        def _():
+            row = slots_ref[slot]
+            for src, dst in ((acts_ref, xs), (cot_ref, gs)):
+                board = src[row].astype(f32)
+                for line in range(BOARD):
+                    dst[pl.ds(inner(line) + slot, BOARD, stride=SLOTS), :] = board[
+                        line * BOARD : (line + 1) * BOARD
+                    ]
+
+    def bias(at):
+        return (
+            weight_ref[2 * taps : 2 * taps + 16, :].astype(f32)[at : at + 3].sum(axis=0, keepdims=True)
+        )
+
+    def wide(lhs, rhs):
+        return lax.dot_general(lhs, rhs, (((1,), (1,)), ((), ())), preferred_element_type=f32)
+
+    def send_rows(which, flat, ref):
+        for slot in range(SLOTS):
+
+            @pl.when(slot < count)
+            def _():
+                stage[which * SLOTS + slot] = flat[pl.ds(slot, CELLS, stride=SLOTS), :].astype(bf16)
+                pltpu.make_async_copy(
+                    stage.at[which * SLOTS + slot],
+                    ref.at[slots_ref[slot]],
+                    sems.at[which * SLOTS + slot],
+                ).start()
+
+    fill_patches(xs, px, channels)
+    pre = jnp.dot(px[...], weight_ref[:taps, :], preferred_element_type=f32) + bias(0)
+    fill_patches(gs, pq, channels)
+    hidden_grad = wide(pq[...], flipped_wide(weight_ref, taps, channels))
+    gate = 0.5 * jnp.tanh(0.5 * pre) + 0.5
+    slope[...] = hidden_grad * (gate * (1.0 + pre * (1.0 - gate)))
+    hidden = (pre * gate).astype(bf16).astype(f32)
+    for line in range(BOARD):
+        hs[inner(line) : inner(line) + LINE, :] = hidden[line * LINE : (line + 1) * LINE]
+    fill_patches(hs, ph, channels)
+
+    flat_out[...] = jnp.dot(ph[...], weight_ref[taps : 2 * taps, :], preferred_element_type=f32) + bias(3)
+    for line in range(BOARD):
+        flat_out[line * LINE : (line + 1) * LINE, :] += xs[inner(line) : inner(line) + LINE, :]
+
+    def weight_grad(grad, patch_ref, base):
+        turned = wide_grad(grad, patch_ref)
+        for tap in range(9):
+            grads_ref[base + tap * channels : base + (tap + 1) * channels, :] = turned[
+                :, tap * channels : (tap + 1) * channels
+            ].astype(bf16)
+
+    def wide_grad(grad, patch_ref):
+        return jnp.dot(grad.T.astype(bf16), patch_ref[...], preferred_element_type=f32)
+
+    upstream = jnp.concatenate(
+        [gs[inner(line) : inner(line) + LINE, :] for line in range(BOARD)], axis=0
+    )
+    weight_grad(upstream, ph, taps)
+    bias_two = jnp.sum(upstream, axis=0, keepdims=True)
+
+    pre_grad = slope[...].astype(bf16).astype(f32)
+    for line in range(BOARD):
+        ps[inner(line) : inner(line) + LINE, :] = pre_grad[line * LINE : (line + 1) * LINE]
+    fill_patches(ps, pq, channels)
+    bias_one = jnp.sum(pre_grad, axis=0, keepdims=True)
+    flat_back[...] = wide(pq[...], flipped_wide(weight_ref, 0, channels))
+    for line in range(BOARD):
+        flat_back[line * LINE : (line + 1) * LINE, :] += gs[inner(line) : inner(line) + LINE, :]
+    weight_grad(pre_grad, px, 0)
+
+    place = lax.broadcasted_iota(jnp.int32, (TAIL, channels), 0)
+    tail = jnp.zeros((TAIL, channels), f32)
+    for at, value in ((0, bias_one), (2, bias_two)):
+        high = value.astype(bf16).astype(f32)
+        tail = jnp.where(place == at, high, tail)
+        tail = jnp.where(place == at + 1, value - high, tail)
+    grads_ref[2 * taps :, :] = tail.astype(bf16)
+    send_rows(0, flat_out, out_ref)
+    send_rows(1, flat_back, back_ref)
+
+    for which, ref in ((0, out_ref), (1, back_ref)):
+        for slot in range(SLOTS):
+
+            @pl.when(slot < count)
+            def _():
+                pltpu.make_async_copy(
+                    stage.at[which * SLOTS + slot],
+                    ref.at[slots_ref[slot]],
+                    sems.at[which * SLOTS + slot],
+                ).wait()
+
+
+def tower(slots, acts, cotangent, weight, previous, after):
+    channels = acts.shape[-1]
+    taps = 9 * channels
+    first = previous is None
+    extra = (0 if first else 2) + len(after)
+    vmem = pl.BlockSpec(memory_space=pltpu.VMEM)
+    anywhere = pl.BlockSpec(memory_space=pl.ANY)
+    rows_shape = jax.ShapeDtypeStruct(acts.shape, acts.dtype)
+    board = pltpu.VMEM((SIDE * SIDE * SLOTS, channels), jnp.float32)
+    patch = pltpu.VMEM((ROWS, taps), jnp.bfloat16)
+    square = pltpu.VMEM((ROWS, channels), jnp.float32)
+    flops = 12 * ROWS * taps * channels
+    return pl.pallas_call(
+        functools.partial(tower_kernel, extra),
+        out_shape=(
+            rows_shape,
+            rows_shape,
+            jax.ShapeDtypeStruct((2 * taps + TAIL, channels), jnp.bfloat16),
+        ),
+        in_specs=[pl.BlockSpec(memory_space=pltpu.SMEM), vmem, vmem, vmem]
+        + [anywhere] * extra,
+        out_specs=(anywhere, anywhere, vmem),
+        scratch_shapes=[board] * 4
+        + [patch] * 3
+        + [square] * 3
+        + [
+            pltpu.VMEM((2 * SLOTS, CELLS, channels), jnp.bfloat16),
+            pltpu.SemaphoreType.DMA((2 * SLOTS,)),
+        ],
+        input_output_aliases={} if first else {4: 0, 5: 1},
+        compiler_params=pltpu.CompilerParams(vmem_limit_bytes=40 * 1024 * 1024),
+        cost_estimate=pl.CostEstimate(flops=6 * flops, bytes_accessed=4000000, transcendentals=ROWS * channels),
+        name="tower",
+    )(slots, acts, cotangent, weight, *(() if first else previous), *after)
+
+
+def parts_of(value):
+    high = lax.reduce_precision(value, 8, 7)
+    middle = lax.reduce_precision(value - high, 8, 7)
+    return [high, middle, value - high - middle]
+
+
+def at_home(acts, cotangent, routes, w_first, w_second, b_first, b_second):
+    owners = lax.axis_size("member")
+    copies = lax.axis_size("rep")
+    channels = acts.shape[-1]
+    taps = 9 * channels
+    me = lax.axis_index("member")
+    member_ids = routes.reshape(-1)
+    total = member_ids.shape[0]
+    named = member_ids[None, :] == jnp.arange(owners, dtype=jnp.int32)[:, None]
+    counts = jnp.sum(named.astype(jnp.int32), axis=1)
+    order = jnp.arange(total, dtype=jnp.int32)
+    before = (order[:, None] > order[None, :]) & named[:, None, :]
+    place = jnp.sum(before.astype(jnp.int32), axis=2)
+    hit = named[:, None, :] & (
+        place[:, None, :] == jnp.arange(SLOTS, dtype=jnp.int32)[None, :, None]
+    )
+    rows = jnp.sum(jnp.where(hit, jnp.arange(total, dtype=jnp.int32)[None, None, :], 0), axis=2)
+    table = jnp.concatenate([rows, counts[:, None]], axis=1)
+
+    x = acts.reshape((total,) + acts.shape[2:])
+    g = cotangent.reshape((total,) + acts.shape[2:])
+    pieces = parts_of(b_first) + parts_of(b_second)
+    bias_tile = jnp.concatenate(
+        [piece.astype(jnp.bfloat16) for piece in pieces]
+        + [jnp.zeros((10, channels), jnp.bfloat16)],
+        axis=0,
+    )
+    own = jnp.concatenate([w_first[0], w_second[0], lax.optimization_barrier(bias_tile)], axis=0)
+
+    def swap(value, offset, axis="member"):
+        size = lax.axis_size(axis)
+        return lax.ppermute(value, axis, [(i, i ^ offset) for i in range(size)])
+
+    chips = owners // 2
+    same = [own] + [swap(own, 2 * step) for step in range(1, chips)]
+    other = [swap(value, 1) for value in same]
+    previous = None
+    summed = None
+    after = ()
+    totals = []
+    held = []
+    for step in range(chips):
+        made = {}
+        order = (0, 1) if step == 0 else (1, 0)
+        for side in order:
+            weight = (same, other)[side][step]
+            member = me ^ (2 * step + side)
+            slots = lax.dynamic_index_in_dim(table, member, 0, keepdims=False)
+            out, back, grads = tower(slots, x, g, weight, previous, after)
+            after = ()
+            previous = (out, back)
+            made[side] = grads
+        pair = made[0].astype(jnp.float32) + swap(made[1], 1).astype(jnp.float32)
+        if step == 0:
+            totals.append(pair)
+        else:
+            narrow = pair.astype(jnp.bfloat16)
+            totals.append(swap(narrow, 2 * step).astype(jnp.float32))
+            held.append(narrow)
+        if held:
+            after = (held.pop(),)
+    summed = sum(totals[1:], totals[0])
+
+    rep = lax.axis_index("rep")
+    chunks = summed.reshape(copies, summed.shape[0] // copies, channels)
+    sends = chunks.astype(jnp.bfloat16)
+    mine = lax.dynamic_index_in_dim(chunks, rep, 0, keepdims=False)
+    for far in range(1, copies):
+        sent = lax.dynamic_index_in_dim(sends, rep ^ far, 0, keepdims=False)
+        mine = mine + swap(sent, far, "rep").astype(jnp.float32)
+    mine = mine.astype(jnp.bfloat16)
+    gathered = [mine] + [swap(mine, far, "rep") for far in range(1, copies)]
+    offset = 1
+    while offset < copies:
+        odd = (rep & offset) != 0
+        gathered = [
+            jnp.where(odd, gathered[at ^ offset], gathered[at]) for at in range(copies)
+        ]
+        offset *= 2
+    summed = jnp.concatenate(gathered, axis=0).astype(jnp.float32)
+
+    def turned(part):
+        return jnp.swapaxes(part.reshape(9, channels, channels), 1, 2).reshape(1, taps, channels)
+
+    tail = summed[2 * taps :]
+    return (
+        previous[0].reshape(acts.shape),
+        previous[1].reshape(acts.shape),
+        turned(summed[:taps]),
+        turned(summed[taps : 2 * taps]),
+        (tail[0] + tail[1])[None],
+        (tail[2] + tail[3])[None],
+    )
+
+
 def solution(mesh):
     placed = (
         P(("rep", "member"), None, None, None),
@@ -151,7 +429,7 @@
         P("member", None),
     )
     return jax.shard_map(
-        shards,
+        at_home if mesh.shape["member"] <= 8 else shards,
         mesh=mesh,
         in_specs=placed,
         out_specs=(

time: 169 us -> 125 us (0.74)
  Pallas kernels: 0 us -> 38.7 us
  matrix products: 38.2 us -> 0 us
  waiting for transfers between devices: 65.2 us -> 50 us
  between operations: 14.2 us -> 0.95 us
  blocking collectives: 12.5 us -> 0 us
  local copies, waits for them, and re-layouts: 17.5 us -> 7.49 us
  other arithmetic: 3.95 us -> 8.3 us
  starting transfers between devices: 16.5 us -> 18.7 us
    ppermute x0 -> x20, waiting for transfers between devices: none -> 50 us  [swap(): return lax.ppermute(value, axis, [(i, i ^ offset) for i in range(size)])]
    pallas_call x0 -> x8, Pallas kernels: none -> 38.7 us  [tower(): pl.pallas_call(functools.partial(tower_kernel, extra), out_shape=(rows_sh...]
    psum x1 -> x0, waiting for transfers between devices: 36.6 us -> none  [shards(): totals = lax.psum((grad_one, grad_two, bias_one, bias_two), 'rep')]
    all_to_all x4 -> x0, waiting for transfers between devices: 28.7 us -> none  [the longest x1 19.8 us: shards(): lax.all_to_all(send_acts, 'member', split_axis=0, concat_axis=0, tiled=True)]
    conv_general_dilated x4 -> x0, matrix products: 20.4 us -> none  [board_conv(): lax.conv_general_dilated(boards, kernel, (1, 1), ((1, 1), (1, 1)), dimens...]
    ppermute x0 -> x20, starting transfers between devices: none -> 18.7 us  [swap(): return lax.ppermute(value, axis, [(i, i ^ offset) for i in range(size)])]
    all_to_all x4 -> x0, starting transfers between devices: 16.2 us -> none  [the longest x1 5.3 us: shards(): lax.all_to_all(send_acts, 'member', split_axis=0, concat_axis=0, tiled=True)]
    psum x1 -> x0, blocking collectives: 12.5 us -> none  [shards(): totals = lax.psum((grad_one, grad_two, bias_one, bias_two), 'rep')]
  transfers between devices with their start and end apart: 5 -> 20, of which waited for: 4 -> 7; matrix products, arithmetic and copies ran while one was open for 30% -> 5% of each run, Pallas kernels for 0% -> 31%
where the time goes in v1:
time: 125 us; the launch traced here: 124 us
  waiting for transfers between devices  50 us (40%)
  Pallas kernels  38.7 us (31%)
  starting transfers between devices  18.7 us (15%)
  other arithmetic  8.3 us (7%)
  local copies, waits for them, and re-layouts  7.49 us (6%)
    ppermute x20, waiting for transfers between devices, swap(): return lax.ppermute(value, axis, [(i, i ^ offset) for i in range(size)])  50 us
    pallas_call x8, Pallas kernels, tower(): pl.pallas_call(functools.partial(tower_kernel, extra), out_shape=(rows_sh...  38.7 us
    ppermute x20, starting transfers between devices, swap(): return lax.ppermute(value, axis, [(i, i ^ offset) for i in range(size)])  18.7 us
    unnamed x17, local copies, waits for them, and re-layouts  4.2 us
  transfers between devices with their start and end apart: 20, of which 7 were waited for; matrix products, arithmetic and copies ran while one was open for 5% of the time, Pallas kernels for 31%

profile of v1, /device:TPU:0, one launch (start us, length us, event | category | flops | bytes accessed | tf_op | source)
XLA Modules:
  0.0 124.1 jit_solution(1303325109456971725)
XLA Ops:
  0.7 0.8 fusion.4
  1.4 0.1 concatenate.13
  1.6 2.0 %pad_maximum_fusion.weight_ref = bf16[2320,128]{1,0:T(8,128)(2,1)} fusion(bf16[16,128]{1,0:T(8,128)(2,1)S(1)} %concatenate.13, bf16[1152,128]{1,0:T(8,128)(2,1)} %bitcast.70, bf16[1152,128]{1,0:T(8,128)(2,1)} %bitcast.71), kind=kLoop, calls=%fused_computation.5 | loop fusion | flops 1781760 | bytes 1187840 | tf_op jit(solution)/shard_map/concatenate | solution.py:353
  3.6 0.5 collective-permute-start.6
  4.0 2.5 %collective-permute-start.4 = (bf16[2320,128]{1,0:T(8,128)(2,1)}, bf16[2320,128]{1,0:T(8,128)(2,1)}, u32[]{:S(2)}, u32[]{:S(2)}) collective-permute-start(bf16[2320,128]{1,0:T(8,128)(2,1)} %pad_maximum_fusion.weight_ref), channel_id=1, source_target_pairs={{0,2},{1,3},{2,0},{3,1},{4,6},{5,7},{6,4},{7,5},{8,10},{9,11},{10,... | collective-permute-start | bytes 1781768 | tf_op jit(solution)/shard_map/ppermute | solution.py:357
  6.5 1.5 %collective-permute-start.2 = (bf16[2320,128]{1,0:T(8,128)(2,1)}, bf16[2320,128]{1,0:T(8,128)(2,1)}, u32[]{:S(2)}, u32[]{:S(2)}) collective-permute-start(bf16[2320,128]{1,0:T(8,128)(2,1)} %pad_maximum_fusion.weight_ref), channel_id=1, source_target_pairs={{0,4},{1,5},{2,6},{3,7},{4,0},{5,1},{6,2},{7,3},{8,12},{9,13},{10,... | collective-permute-start | bytes 1781768 | tf_op jit(solution)/shard_map/ppermute | solution.py:357
  8.2 0.1 convert_reduce_fusion.1
  8.3 0.2 convert_reduce_fusion
  8.6 0.2 select_reduce_fusion
  8.9 0.1 copy.45
  9.3 4.8 %tower.8 = (bf16[32,100,128]{2,1,0:T(8,128)(2,1)S(1)}, bf16[32,100,128]{2,1,0:T(8,128)(2,1)S(1)}, bf16[2368,128]{1,0:T(8,128)(2,1)S(1)}) custom-call(s32[9]{0:T(128)S(1)} %get-tuple-element.83.slots_ref, bf16[32,100,128]{2,1,0:T(8,128)(2,1)S(1)} %bitcast.46, bf16[32,100,128]{2,1,0:T(8,128)(2,1)S(1)} %bitcast.54, bf16[2320,128]{1,0:T(8,128)(2,1)} %pad_maximum_fusion.weight_ref), custom_call_target="tpu_custom_call" | custom-call | flops 8493465600 | bytes 4000000 | tf_op jit(solution)/shard_map/tower/pallas_call | solution.py:296
  14.0 7.0 %collective-permute-done.4.weight_ref = bf16[2320,128]{1,0:T(8,128)(2,1)} collective-permute-done((bf16[2320,128]{1,0:T(8,128)(2,1)}, bf16[2320,128]{1,0:T(8,128)(2,1)}, u32[]{:S(2)}, u32[]{:S(2)}) %collective-permute-start.4) | collective-permute-done | bytes 593952 | tf_op jit(solution)/shard_map/ppermute | solution.py:357
  21.1 5.5 %tower.9 = (bf16[32,100,128]{2,1,0:T(8,128)(2,1)S(1)}, bf16[32,100,128]{2,1,0:T(8,128)(2,1)S(1)}, bf16[2368,128]{1,0:T(8,128)(2,1)}) custom-call(s32[9]{0:T(128)S(1)} %get-tuple-element.84.slots_ref, bf16[32,100,128]{2,1,0:T(8,128)(2,1)S(1)} %bitcast.47, bf16[32,100,128]{2,1,0:T(8,128)(2,1)S(1)} %bitcast.55, ...), custom_call_target="tpu_custom_call", output_to_operand_aliasing={{0}: (4, {}), {1}: (5, {})} | custom-call | flops 8493465600 | bytes 4000000 | tf_op jit(solution)/shard_map/tower/pallas_call | solution.py:296
  26.6 0.9 collective-permute-start.9
  27.5 7.6 %collective-permute-done.2.weight_ref = bf16[2320,128]{1,0:T(8,128)(2,1)} collective-permute-done((bf16[2320,128]{1,0:T(8,128)(2,1)}, bf16[2320,128]{1,0:T(8,128)(2,1)}, u32[]{:S(2)}, u32[]{:S(2)}) %collective-permute-start.2) | collective-permute-done | bytes 593952 | tf_op jit(solution)/shard_map/ppermute | solution.py:357
  35.1 0.5 collective-permute-start.1
  35.6 4.6 %tower.10 = (bf16[32,100,128]{2,1,0:T(8,128)(2,1)S(1)}, bf16[32,100,128]{2,1,0:T(8,128)(2,1)S(1)}, bf16[2368,128]{1,0:T(8,128)(2,1)S(1)}) custom-call(s32[9]{0:T(128)S(1)} %get-tuple-element.85.slots_ref, bf16[32,100,128]{2,1,0:T(8,128)(2,1)S(1)} %bitcast.48, bf16[32,100,128]{2,1,0:T(8,128)(2,1)S(1)} %bitcast.56, ...), custom_call_target="tpu_custom_call", output_to_operand_aliasing={{0}: (4, {}), {1}: (5, {})} | custom-call | flops 8493465600 | bytes 4000000 | tf_op jit(solution)/shard_map/tower/pallas_call | solution.py:296
  40.3 4.9 %tower.11 = (bf16[32,100,128]{2,1,0:T(8,128)(2,1)S(1)}, bf16[32,100,128]{2,1,0:T(8,128)(2,1)S(1)}, bf16[2368,128]{1,0:T(8,128)(2,1)S(1)}) custom-call(s32[9]{0:T(128)S(1)} %get-tuple-element.86.slots_ref, bf16[32,100,128]{2,1,0:T(8,128)(2,1)S(1)} %bitcast.49, bf16[32,100,128]{2,1,0:T(8,128)(2,1)S(1)} %bitcast.57, ...), custom_call_target="tpu_custom_call", output_to_operand_aliasing={{0}: (4, {}), {1}: (5, {})} | custom-call | flops 8493465600 | bytes 4000000 | tf_op jit(solution)/shard_map/tower/pallas_call | solution.py:296
  45.2 1.0 add_convert_fusion.2.rest_2_
  46.2 0.7 collective-permute-start.10
  47.0 4.1 %tower.12 = (bf16[32,100,128]{2,1,0:T(8,128)(2,1)S(1)}, bf16[32,100,128]{2,1,0:T(8,128)(2,1)S(1)}, bf16[2368,128]{1,0:T(8,128)(2,1)S(1)}) custom-call(s32[9]{0:T(128)S(1)} %get-tuple-element.87.slots_ref, bf16[32,100,128]{2,1,0:T(8,128)(2,1)S(1)} %bitcast.50, bf16[32,100,128]{2,1,0:T(8,128)(2,1)S(1)} %bitcast.58, ...), custom_call_target="tpu_custom_call", output_to_operand_aliasing={{0}: (4, {}), {1}: (5, {})} | custom-call | flops 8493465600 | bytes 4000000 | tf_op jit(solution)/shard_map/tower/pallas_call | solution.py:296
  51.1 0.4 collective-permute-start.8
  51.5 5.4 %tower.13 = (bf16[32,100,128]{2,1,0:T(8,128)(2,1)S(1)}, bf16[32,100,128]{2,1,0:T(8,128)(2,1)S(1)}, bf16[2368,128]{1,0:T(8,128)(2,1)S(1)}) custom-call(s32[9]{0:T(128)S(1)} %get-tuple-element.88.slots_ref, bf16[32,100,128]{2,1,0:T(8,128)(2,1)S(1)} %bitcast.51, bf16[32,100,128]{2,1,0:T(8,128)(2,1)S(1)} %bitcast.59, ...), custom_call_target="tpu_custom_call", output_to_operand_aliasing={{0}: (4, {}), {1}: (5, {})} | custom-call | flops 8493465600 | bytes 4000000 | tf_op jit(solution)/shard_map/tower/pallas_call | solution.py:296
  56.9 1.0 add_convert_fusion.1.rest_2_
  57.9 1.2 collective-permute-start.11
  59.1 4.8 %tower.14 = (bf16[32,100,128]{2,1,0:T(8,128)(2,1)S(1)}, bf16[32,100,128]{2,1,0:T(8,128)(2,1)S(1)}, bf16[2368,128]{1,0:T(8,128)(2,1)S(1)}) custom-call(s32[9]{0:T(128)S(1)} %get-tuple-element.89.slots_ref, bf16[32,100,128]{2,1,0:T(8,128)(2,1)S(1)} %bitcast.52, bf16[32,100,128]{2,1,0:T(8,128)(2,1)S(1)} %bitcast.60, ...), custom_call_target="tpu_custom_call", output_to_operand_aliasing={{0}: (4, {}), {1}: (5, {})} | custom-call | flops 8493465600 | bytes 4000000 | tf_op jit(solution)/shard_map/tower/pallas_call | solution.py:296
  64.0 4.6 %tower.15 = (bf16[32,100,128]{2,1,0:T(8,128)(2,1)S(1)}, bf16[32,100,128]{2,1,0:T(8,128)(2,1)S(1)}, bf16[2368,128]{1,0:T(8,128)(2,1)S(1)}) custom-call(s32[9]{0:T(128)S(1)} %get-tuple-element.90.slots_ref, bf16[32,100,128]{2,1,0:T(8,128)(2,1)S(1)} %bitcast.53, bf16[32,100,128]{2,1,0:T(8,128)(2,1)S(1)} %bitcast.61, ...), custom_call_target="tpu_custom_call", output_to_operand_aliasing={{0}: (4, {}), {1}: (5, {})} | custom-call | flops 8493465600 | bytes 4000000 | tf_op jit(solution)/shard_map/tower/pallas_call | solution.py:296
  68.7 0.2 add_convert_fusion
  68.8 1.5 %collective-permute-start.13 = (bf16[2368,128]{1,0:T(8,128)(2,1)S(1)}, bf16[2368,128]{1,0:T(8,128)(2,1)S(1)}, u32[]{:S(2)}, u32[]{:S(2)}) collective-permute-start(bf16[2368,128]{1,0:T(8,128)(2,1)S(1)} %add_convert_fusion), channel_id=1, source_target_pairs={{0,6},{1,7},{2,4},{3,5},{4,2},{5,3},{6,0},{7,1},{8,14},{9,15},{10,... | collective-permute-start | bytes 1818632 | tf_op jit(solution)/shard_map/ppermute | solution.py:357
  70.3 16.7 %collective-permute-done.11 = bf16[2368,128]{1,0:T(8,128)(2,1)} collective-permute-done((bf16[2368,128]{1,0:T(8,128)(2,1)}, bf16[2368,128]{1,0:T(8,128)(2,1)}, u32[]{:S(2)}, u32[]{:S(2)}) %collective-permute-start.11) | collective-permute-done | bytes 606240 | tf_op jit(solution)/shard_map/ppermute | solution.py:357
  87.0 0.8 copy-done.4
  87.8 2.0 %convert_add_fusion = f32[2368,128]{1,0:T(8,128)S(1)} fusion(bf16[2368,128]{1,0:T(8,128)(2,1)} %copy-done.4, bf16[2368,128]{1,0:T(8,128)(2,1)} %collective-permute-done.11, bf16[2368,128]{1,0:T(8,128)(2,1)} %collective-permute-done.10, bf16[2368,128]{1,0:T(8,128)(2,1)} %collective-permute-done.9, bf16[2368,128]{1,0:T(8,128)(2,1)S(1)} %copy-done.1), kind=kLoop, calls=%fused_computation | loop fusion | flops 2727936 | bytes 4243456 | tf_op jit(solution)/shard_map/add | solution.py:387
  89.9 0.8 dynamic-slice_bitcast_fusion.2
  90.7 1.2 collective-permute-start.14
  91.9 2.5 %collective-permute-start.15 = (bf16[592,128]{1,0:T(8,128)(2,1)}, bf16[592,128]{1,0:T(8,128)(2,1)S(1)}, u32[]{:S(2)}, u32[]{:S(2)}) collective-permute-start(bf16[592,128]{1,0:T(8,128)(2,1)} %get-tuple-element.82), channel_id=1, source_target_pairs={{0,16},{8,24},{16,0},{24,8},{1,17},{9,25},{17,1},{25,9},{2,18},{10... | collective-permute-start | bytes 454664 | tf_op jit(solution)/shard_map/ppermute | solution.py:357
  94.4 0.7 collective-permute-start.16
  95.0 3.1 %collective-permute-done.14 = bf16[592,128]{1,0:T(8,128)(2,1)S(1)} collective-permute-done((bf16[592,128]{1,0:T(8,128)(2,1)}, bf16[592,128]{1,0:T(8,128)(2,1)S(1)}, u32[]{:S(2)}, u32[]{:S(2)}) %collective-permute-start.14) | collective-permute-done | bytes 151584 | tf_op jit(solution)/shard_map/ppermute | solution.py:357
  98.2 8.2 %collective-permute-done.15 = bf16[592,128]{1,0:T(8,128)(2,1)S(1)} collective-permute-done((bf16[592,128]{1,0:T(8,128)(2,1)}, bf16[592,128]{1,0:T(8,128)(2,1)S(1)}, u32[]{:S(2)}, u32[]{:S(2)}) %collective-permute-start.15) | collective-permute-done | bytes 151584 | tf_op jit(solution)/shard_map/ppermute | solution.py:357
  106.4 2.4 %collective-permute-start.17 = (bf16[592,128]{1,0:T(8,128)(2,1)S(1)}, bf16[592,128]{1,0:T(8,128)(2,1)S(1)}, u32[]{:S(2)}, u32[]{:S(2)}) collective-permute-start(bf16[592,128]{1,0:T(8,128)(2,1)S(1)} %fusion.2), channel_id=1, source_target_pairs={{0,24},{8,16},{16,8},{24,0},{1,25},{9,17},{17,9},{25,1},{2,26},{10... | collective-permute-start | bytes 454664 | tf_op jit(solution)/shard_map/ppermute | solution.py:357
  108.9 1.6 %collective-permute-start.18 = (bf16[592,128]{1,0:T(8,128)(2,1)S(1)}, bf16[592,128]{1,0:T(8,128)(2,1)S(1)}, u32[]{:S(2)}, u32[]{:S(2)}) collective-permute-start(bf16[592,128]{1,0:T(8,128)(2,1)S(1)} %fusion.2), channel_id=1, source_target_pairs={{0,16},{8,24},{16,0},{24,8},{1,17},{9,25},{17,1},{25,9},{2,18},{10... | collective-permute-start | bytes 454664 | tf_op jit(solution)/shard_map/ppermute | solution.py:357
  110.4 0.4 collective-permute-start.19
  110.9 1.5 %copy.49 = bf16[16,2,100,128]{3,1,2,0:T(2,128)(2,1)} copy(bf16[16,2,100,128]{3,2,1,0:T(8,128)(2,1)S(1)} %bitcast.62) | data formatting | bytes 1638400
  112.4 1.5 %copy.50 = bf16[16,2,100,128]{3,1,2,0:T(2,128)(2,1)} copy(bf16[16,2,100,128]{3,2,1,0:T(8,128)(2,1)S(1)} %bitcast.63) | data formatting | bytes 1638400
  113.9 1.3 %collective-permute-done.17 = bf16[592,128]{1,0:T(8,128)(2,1)S(1)} collective-permute-done((bf16[592,128]{1,0:T(8,128)(2,1)S(1)}, bf16[592,128]{1,0:T(8,128)(2,1)S(1)}, u32[]{:S(2)}, u32[]{:S(2)}) %collective-permute-start.17) | collective-permute-done | bytes 151584 | tf_op jit(solution)/shard_map/ppermute | solution.py:357
  115.2 6.0 %collective-permute-done.18 = bf16[592,128]{1,0:T(8,128)(2,1)S(1)} collective-permute-done((bf16[592,128]{1,0:T(8,128)(2,1)S(1)}, bf16[592,128]{1,0:T(8,128)(2,1)S(1)}, u32[]{:S(2)}, u32[]{:S(2)}) %collective-permute-start.18) | collective-permute-done | bytes 151584 | tf_op jit(solution)/shard_map/ppermute | solution.py:357
  121.3 0.5 convert_add_fusion.1
  122.0 1.1 copy.47
  123.1 1.0 copy.48
  (43 shorter events, 1.1 us)
Async XLA Ops:
  0.6 7.4 %copy-start.5 = (s32[16,2]{0,1:T(2,128)S(1)}, s32[16,2]{0,1:T(2,128)}, u32[]{:S(2)}) copy-start(s32[16,2]{0,1:T(2,128)} %param.9) | copy-start | bytes 388
  0.6 8.2 %copy-start.2 = (bf16[16,2,100,128]{3,1,2,0:T(2,128)(2,1)S(1)}, bf16[16,2,100,128]{3,1,2,0:T(2,128)(2,1)}, u32[]{:S(2)}) copy-start(bf16[16,2,100,128]{3,1,2,0:T(2,128)(2,1)} %param.7) | copy-start | bytes 2457604
  1.6 7.4 %copy-start.3 = (bf16[16,2,100,128]{3,1,2,0:T(2,128)(2,1)S(1)}, bf16[16,2,100,128]{3,1,2,0:T(2,128)(2,1)}, u32[]{:S(2)}) copy-start(bf16[16,2,100,128]{3,1,2,0:T(2,128)(2,1)} %param.8) | copy-start | bytes 2457604
  3.6 17.5 %collective-permute-start.6 = (bf16[2320,128]{1,0:T(8,128)(2,1)}, bf16[2320,128]{1,0:T(8,128)(2,1)}, u32[]{:S(2)}, u32[]{:S(2)}) collective-permute-start(bf16[2320,128]{1,0:T(8,128)(2,1)} %pad_maximum_fusion.weight_ref), channel_id=1, source_target_pairs={{0,1},{1,0},{2,3},{3,2},{4,5},{5,4},{6,7},{7,6},{8,9},{9,8},{10,11... | collective-permute-start | bytes 1781768 | tf_op jit(solution)/shard_map/ppermute | solution.py:357
  4.0 17.1 %collective-permute-start.4 = (bf16[2320,128]{1,0:T(8,128)(2,1)}, bf16[2320,128]{1,0:T(8,128)(2,1)}, u32[]{:S(2)}, u32[]{:S(2)}) collective-permute-start(bf16[2320,128]{1,0:T(8,128)(2,1)} %pad_maximum_fusion.weight_ref), channel_id=1, source_target_pairs={{0,2},{1,3},{2,0},{3,1},{4,6},{5,7},{6,4},{7,5},{8,10},{9,11},{10,... | collective-permute-start | bytes 1781768 | tf_op jit(solution)/shard_map/ppermute | solution.py:357
  6.5 28.6 %collective-permute-start.2 = (bf16[2320,128]{1,0:T(8,128)(2,1)}, bf16[2320,128]{1,0:T(8,128)(2,1)}, u32[]{:S(2)}, u32[]{:S(2)}) collective-permute-start(bf16[2320,128]{1,0:T(8,128)(2,1)} %pad_maximum_fusion.weight_ref), channel_id=1, source_target_pairs={{0,4},{1,5},{2,6},{3,7},{4,0},{5,1},{6,2},{7,3},{8,12},{9,13},{10,... | collective-permute-start | bytes 1781768 | tf_op jit(solution)/shard_map/ppermute | solution.py:357
  8.0 27.1 %collective-permute-start = (bf16[2320,128]{1,0:T(8,128)(2,1)}, bf16[2320,128]{1,0:T(8,128)(2,1)}, u32[]{:S(2)}, u32[]{:S(2)}) collective-permute-start(bf16[2320,128]{1,0:T(8,128)(2,1)} %pad_maximum_fusion.weight_ref), channel_id=1, source_target_pairs={{0,6},{1,7},{2,4},{3,5},{4,2},{5,3},{6,0},{7,1},{8,14},{9,15},{10,... | collective-permute-start | bytes 1781768 | tf_op jit(solution)/shard_map/ppermute | solution.py:357
  14.0 12.5 %copy-start = (bf16[2368,128]{1,0:T(8,128)(2,1)}, bf16[2368,128]{1,0:T(8,128)(2,1)S(1)}, u32[]{:S(2)}) copy-start(bf16[2368,128]{1,0:T(8,128)(2,1)S(1)} %get-tuple-element.50) | copy-start | bytes 1818628
  21.1 14.5 %collective-permute-start.5 = (bf16[2320,128]{1,0:T(8,128)(2,1)}, bf16[2320,128]{1,0:T(8,128)(2,1)S(1)}, u32[]{:S(2)}, u32[]{:S(2)}) collective-permute-start(bf16[2320,128]{1,0:T(8,128)(2,1)} %collective-permute-done.4.weight_ref), channel_id=1, source_target_pairs={{0,1},{1,0},{2,3},{3,2},{4,5},{5,4},{6,7},{7,6},{8,9},{9,8},{10,11... | collective-permute-start | bytes 1781768 | tf_op jit(solution)/shard_map/ppermute | solution.py:357
  26.6 43.7 %collective-permute-start.9 = (bf16[2368,128]{1,0:T(8,128)(2,1)}, bf16[2368,128]{1,0:T(8,128)(2,1)}, u32[]{:S(2)}, u32[]{:S(2)}) collective-permute-start(bf16[2368,128]{1,0:T(8,128)(2,1)} %get-tuple-element.51), channel_id=1, source_target_pairs={{0,1},{1,0},{2,3},{3,2},{4,5},{5,4},{6,7},{7,6},{8,9},{9,8},{10,11... | collective-permute-start | bytes 1818632 | tf_op jit(solution)/shard_map/ppermute | solution.py:357
  35.1 11.9 %collective-permute-start.3 = (bf16[2320,128]{1,0:T(8,128)(2,1)}, bf16[2320,128]{1,0:T(8,128)(2,1)S(1)}, u32[]{:S(2)}, u32[]{:S(2)}) collective-permute-start(bf16[2320,128]{1,0:T(8,128)(2,1)} %collective-permute-done.2.weight_ref), channel_id=1, source_target_pairs={{0,1},{1,0},{2,3},{3,2},{4,5},{5,4},{6,7},{7,6},{8,9},{9,8},{10,11... | collective-permute-start | bytes 1781768 | tf_op jit(solution)/shard_map/ppermute | solution.py:357
  35.1 24.0 %collective-permute-start.1 = (bf16[2320,128]{1,0:T(8,128)(2,1)}, bf16[2320,128]{1,0:T(8,128)(2,1)S(1)}, u32[]{:S(2)}, u32[]{:S(2)}) collective-permute-start(bf16[2320,128]{1,0:T(8,128)(2,1)} %collective-permute-done.weight_ref), channel_id=1, source_target_pairs={{0,1},{1,0},{2,3},{3,2},{4,5},{5,4},{6,7},{7,6},{8,9},{9,8},{10,11... | collective-permute-start | bytes 1781768 | tf_op jit(solution)/shard_map/ppermute | solution.py:357
  40.3 5.0 %collective-permute-start.7 = (bf16[2368,128]{1,0:T(8,128)(2,1)S(1)}, bf16[2368,128]{1,0:T(8,128)(2,1)S(1)}, u32[]{:S(2)}, u32[]{:S(2)}) collective-permute-start(bf16[2368,128]{1,0:T(8,128)(2,1)S(1)} %get-tuple-element.39), channel_id=1, source_target_pairs={{0,1},{1,0},{2,3},{3,2},{4,5},{5,4},{6,7},{7,6},{8,9},{9,8},{10,11... | collective-permute-start | bytes 1818632 | tf_op jit(solution)/shard_map/ppermute | solution.py:357
  46.2 24.1 %collective-permute-start.10 = (bf16[2368,128]{1,0:T(8,128)(2,1)}, bf16[2368,128]{1,0:T(8,128)(2,1)}, u32[]{:S(2)}, u32[]{:S(2)}) collective-permute-start(bf16[2368,128]{1,0:T(8,128)(2,1)} %add_convert_fusion.2.rest_2_), channel_id=1, source_target_pairs={{0,2},{1,3},{2,0},{3,1},{4,6},{5,7},{6,4},{7,5},{8,10},{9,11},{10,... | collective-permute-start | bytes 1818632 | tf_op jit(solution)/shard_map/ppermute | solution.py:357
  51.1 5.8 %collective-permute-start.8 = (bf16[2368,128]{1,0:T(8,128)(2,1)S(1)}, bf16[2368,128]{1,0:T(8,128)(2,1)S(1)}, u32[]{:S(2)}, u32[]{:S(2)}) collective-permute-start(bf16[2368,128]{1,0:T(8,128)(2,1)S(1)} %get-tuple-element.45), channel_id=1, source_target_pairs={{0,1},{1,0},{2,3},{3,2},{4,5},{5,4},{6,7},{7,6},{8,9},{9,8},{10,11... | collective-permute-start | bytes 1818632 | tf_op jit(solution)/shard_map/ppermute | solution.py:357
  57.9 29.1 %collective-permute-start.11 = (bf16[2368,128]{1,0:T(8,128)(2,1)}, bf16[2368,128]{1,0:T(8,128)(2,1)}, u32[]{:S(2)}, u32[]{:S(2)}) collective-permute-start(bf16[2368,128]{1,0:T(8,128)(2,1)} %add_convert_fusion.1.rest_2_), channel_id=1, source_target_pairs={{0,4},{1,5},{2,6},{3,7},{4,0},{5,1},{6,2},{7,3},{8,12},{9,13},{10,... | collective-permute-start | bytes 1818632 | tf_op jit(solution)/shard_map/ppermute | solution.py:357
  63.9 4.7 %collective-permute-start.12 = (bf16[2368,128]{1,0:T(8,128)(2,1)S(1)}, bf16[2368,128]{1,0:T(8,128)(2,1)S(1)}, u32[]{:S(2)}, u32[]{:S(2)}) collective-permute-start(bf16[2368,128]{1,0:T(8,128)(2,1)S(1)} %get-tuple-element.53), channel_id=1, source_target_pairs={{0,1},{1,0},{2,3},{3,2},{4,5},{5,4},{6,7},{7,6},{8,9},{9,8},{10,11... | collective-permute-start | bytes 1818632 | tf_op jit(solution)/shard_map/ppermute | solution.py:357
  68.7 19.2 %copy-start.1 = (bf16[2368,128]{1,0:T(8,128)(2,1)S(1)}, bf16[2368,128]{1,0:T(8,128)(2,1)}, u32[]{:S(2)}) copy-start(bf16[2368,128]{1,0:T(8,128)(2,1)} %copy-done) | copy-start | bytes 1818628
  68.8 18.1 %collective-permute-start.13 = (bf16[2368,128]{1,0:T(8,128)(2,1)S(1)}, bf16[2368,128]{1,0:T(8,128)(2,1)S(1)}, u32[]{:S(2)}, u32[]{:S(2)}) collective-permute-start(bf16[2368,128]{1,0:T(8,128)(2,1)S(1)} %add_convert_fusion), channel_id=1, source_target_pairs={{0,6},{1,7},{2,4},{3,5},{4,2},{5,3},{6,0},{7,1},{8,14},{9,15},{10,... | collective-permute-start | bytes 1818632 | tf_op jit(solution)/shard_map/ppermute | solution.py:357
  87.0 0.8 copy-start.4
  90.7 7.5 %collective-permute-start.14 = (bf16[592,128]{1,0:T(8,128)(2,1)}, bf16[592,128]{1,0:T(8,128)(2,1)S(1)}, u32[]{:S(2)}, u32[]{:S(2)}) collective-permute-start(bf16[592,128]{1,0:T(8,128)(2,1)} %get-tuple-element.80), channel_id=1, source_target_pairs={{0,8},{8,0},{16,24},{24,16},{1,9},{9,1},{17,25},{25,17},{2,10},{10... | collective-permute-start | bytes 454664 | tf_op jit(solution)/shard_map/ppermute | solution.py:357
  91.9 14.5 %collective-permute-start.15 = (bf16[592,128]{1,0:T(8,128)(2,1)}, bf16[592,128]{1,0:T(8,128)(2,1)S(1)}, u32[]{:S(2)}, u32[]{:S(2)}) collective-permute-start(bf16[592,128]{1,0:T(8,128)(2,1)} %get-tuple-element.82), channel_id=1, source_target_pairs={{0,16},{8,24},{16,0},{24,8},{1,17},{9,25},{17,1},{25,9},{2,18},{10... | collective-permute-start | bytes 454664 | tf_op jit(solution)/shard_map/ppermute | solution.py:357
  94.4 12.0 %collective-permute-start.16 = (bf16[592,128]{1,0:T(8,128)(2,1)}, bf16[592,128]{1,0:T(8,128)(2,1)S(1)}, u32[]{:S(2)}, u32[]{:S(2)}) collective-permute-start(bf16[592,128]{1,0:T(8,128)(2,1)} %get-tuple-element.81), channel_id=1, source_target_pairs={{0,24},{8,16},{16,8},{24,0},{1,25},{9,17},{17,9},{25,1},{2,26},{10... | collective-permute-start | bytes 454664 | tf_op jit(solution)/shard_map/ppermute | solution.py:357
  106.4 8.8 %collective-permute-start.17 = (bf16[592,128]{1,0:T(8,128)(2,1)S(1)}, bf16[592,128]{1,0:T(8,128)(2,1)S(1)}, u32[]{:S(2)}, u32[]{:S(2)}) collective-permute-start(bf16[592,128]{1,0:T(8,128)(2,1)S(1)} %fusion.2), channel_id=1, source_target_pairs={{0,24},{8,16},{16,8},{24,0},{1,25},{9,17},{17,9},{25,1},{2,26},{10... | collective-permute-start | bytes 454664 | tf_op jit(solution)/shard_map/ppermute | solution.py:357
  108.9 12.4 %collective-permute-start.18 = (bf16[592,128]{1,0:T(8,128)(2,1)S(1)}, bf16[592,128]{1,0:T(8,128)(2,1)S(1)}, u32[]{:S(2)}, u32[]{:S(2)}) collective-permute-start(bf16[592,128]{1,0:T(8,128)(2,1)S(1)} %fusion.2), channel_id=1, source_target_pairs={{0,16},{8,24},{16,0},{24,8},{1,17},{9,25},{17,1},{25,9},{2,18},{10... | collective-permute-start | bytes 454664 | tf_op jit(solution)/shard_map/ppermute | solution.py:357
  110.4 10.8 %collective-permute-start.19 = (bf16[592,128]{1,0:T(8,128)(2,1)S(1)}, bf16[592,128]{1,0:T(8,128)(2,1)S(1)}, u32[]{:S(2)}, u32[]{:S(2)}) collective-permute-start(bf16[592,128]{1,0:T(8,128)(2,1)S(1)} %fusion.2), channel_id=1, source_target_pairs={{0,8},{8,0},{16,24},{24,16},{1,9},{9,1},{17,25},{25,17},{2,10},{10... | collective-permute-start | bytes 454664 | tf_op jit(solution)/shard_map/ppermute | solution.py:357

commit v2 on v1

--- a/solution.py
+++ b/solution.py
@@ -364,6 +364,7 @@
     after = ()
     totals = []
     held = []
+    last = None
     for step in range(chips):
         made = {}
         order = (0, 1) if step == 0 else (1, 0)
@@ -378,21 +379,30 @@
         pair = made[0].astype(jnp.float32) + swap(made[1], 1).astype(jnp.float32)
         if step == 0:
             totals.append(pair)
+        elif step == chips - 1:
+            last = pair
         else:
             narrow = pair.astype(jnp.bfloat16)
             totals.append(swap(narrow, 2 * step).astype(jnp.float32))
             held.append(narrow)
         if held:
             after = (held.pop(),)
-    summed = sum(totals[1:], totals[0])
 
     rep = lax.axis_index("rep")
-    chunks = summed.reshape(copies, summed.shape[0] // copies, channels)
-    sends = chunks.astype(jnp.bfloat16)
-    mine = lax.dynamic_index_in_dim(chunks, rep, 0, keepdims=False)
-    for far in range(1, copies):
-        sent = lax.dynamic_index_in_dim(sends, rep ^ far, 0, keepdims=False)
-        mine = mine + swap(sent, far, "rep").astype(jnp.float32)
+
+    def scattered(value):
+        chunks = value.reshape(copies, value.shape[0] // copies, channels)
+        sends = chunks.astype(jnp.bfloat16)
+        mine = lax.dynamic_index_in_dim(chunks, rep, 0, keepdims=False)
+        for far in range(1, copies):
+            sent = lax.dynamic_index_in_dim(sends, rep ^ far, 0, keepdims=False)
+            mine = mine + swap(sent, far, "rep").astype(jnp.float32)
+        return mine
+
+    mine = 0.0
+    if last is not None:
+        mine = swap(scattered(last).astype(jnp.bfloat16), 2 * (chips - 1)).astype(jnp.float32)
+    mine = mine + scattered(sum(totals[1:], totals[0]))
     mine = mine.astype(jnp.bfloat16)
     gathered = [mine] + [swap(mine, far, "rep") for far in range(1, copies)]
     offset = 1

time: 125 us -> 116 us (0.928)
  waiting for transfers between devices: 50 us -> 38.7 us
  starting transfers between devices: 18.7 us -> 26.3 us
  other arithmetic: 8.3 us -> 5.1 us
  local copies, waits for them, and re-layouts: 7.49 us -> 5.98 us
    ppermute x20 -> x23, waiting for transfers between devices: 50 us -> 38.7 us  [swap(): return lax.ppermute(value, axis, [(i, i ^ offset) for i in range(size)])]
    ppermute x20 -> x23, starting transfers between devices: 18.7 us -> 26.3 us  [swap(): return lax.ppermute(value, axis, [(i, i ^ offset) for i in range(size)])]
    convert_element_type x3 -> x2, other arithmetic: 2.12 us -> 0.32 us  [at_home(): narrow = pair.astype(jnp.bfloat16)]
    add x1 -> x2, other arithmetic: 1.97 us -> 0.4 us  [the longest x1 0.28 us: at_home(): mine = mine + scattered(sum(totals[1:], totals[0]))]
    unnamed x17 -> x11, local copies, waits for them, and re-layouts: 4.2 us -> 3.37 us
  transfers between devices with their start and end apart: 20 -> 23, of which waited for: 7 -> 7; matrix products, arithmetic and copies ran while one was open for 5% -> 5% of each run, Pallas kernels for 31% -> 33%
where the time goes in v2:
time: 116 us; the launch traced here: 115 us
  waiting for transfers between devices  38.7 us (33%)
  Pallas kernels  37.9 us (33%)
  starting transfers between devices  26.3 us (23%)
  local copies, waits for them, and re-layouts  5.98 us (5%)
  other arithmetic  5.1 us (4%)
    ppermute x23, waiting for transfers between devices, swap(): return lax.ppermute(value, axis, [(i, i ^ offset) for i in range(size)])  38.7 us
    pallas_call x8, Pallas kernels, tower(): pl.pallas_call(functools.partial(tower_kernel, extra), out_shape=(rows_sh...  37.9 us
    ppermute x23, starting transfers between devices, swap(): return lax.ppermute(value, axis, [(i, i ^ offset) for i in range(size)])  26.3 us
    unnamed x11, local copies, waits for them, and re-layouts  3.37 us
  transfers between devices with their start and end apart: 23, of which 7 were waited for; matrix products, arithmetic and copies ran while one was open for 5% of the time, Pallas kernels for 33%

profile of v2, /device:TPU:0, one launch (start us, length us, event | category | flops | bytes accessed | tf_op | source)
XLA Modules:
  0.0 114.9 jit_solution(4677357460272173806)
XLA Ops:
  0.7 0.8 fusion.8
  1.4 0.1 concatenate.13
  1.6 2.0 %pad_maximum_fusion.weight_ref = bf16[2320,128]{1,0:T(8,128)(2,1)} fusion(bf16[16,128]{1,0:T(8,128)(2,1)S(1)} %concatenate.13, bf16[1152,128]{1,0:T(8,128)(2,1)} %bitcast.89, bf16[1152,128]{1,0:T(8,128)(2,1)} %bitcast.90), kind=kLoop, calls=%fused_computation.5 | loop fusion | flops 1781760 | bytes 1187840 | tf_op jit(solution)/shard_map/concatenate | solution.py:353
  3.6 0.5 collective-permute-start.6
  4.0 2.5 %collective-permute-start.4 = (bf16[2320,128]{1,0:T(8,128)(2,1)}, bf16[2320,128]{1,0:T(8,128)(2,1)}, u32[]{:S(2)}, u32[]{:S(2)}) collective-permute-start(bf16[2320,128]{1,0:T(8,128)(2,1)} %pad_maximum_fusion.weight_ref), channel_id=1, source_target_pairs={{0,2},{1,3},{2,0},{3,1},{4,6},{5,7},{6,4},{7,5},{8,10},{9,11},{10,... | collective-permute-start | bytes 1781768 | tf_op jit(solution)/shard_map/ppermute | solution.py:357
  6.5 1.5 %collective-permute-start.2 = (bf16[2320,128]{1,0:T(8,128)(2,1)}, bf16[2320,128]{1,0:T(8,128)(2,1)}, u32[]{:S(2)}, u32[]{:S(2)}) collective-permute-start(bf16[2320,128]{1,0:T(8,128)(2,1)} %pad_maximum_fusion.weight_ref), channel_id=1, source_target_pairs={{0,4},{1,5},{2,6},{3,7},{4,0},{5,1},{6,2},{7,3},{8,12},{9,13},{10,... | collective-permute-start | bytes 1781768 | tf_op jit(solution)/shard_map/ppermute | solution.py:357
  8.2 0.1 convert_reduce_fusion.1
  8.4 0.2 convert_reduce_fusion
  8.6 0.2 select_reduce_fusion
  8.9 0.1 copy.45
  9.0 0.1 copy.46
  9.3 4.9 %tower.8 = (bf16[32,100,128]{2,1,0:T(8,128)(2,1)S(1)}, bf16[32,100,128]{2,1,0:T(8,128)(2,1)S(1)}, bf16[2368,128]{1,0:T(8,128)(2,1)S(1)}) custom-call(s32[9]{0:T(128)S(1)} %get-tuple-element.86.slots_ref, bf16[32,100,128]{2,1,0:T(8,128)(2,1)S(1)} %bitcast.63, bf16[32,100,128]{2,1,0:T(8,128)(2,1)S(1)} %bitcast.71, bf16[2320,128]{1,0:T(8,128)(2,1)} %pad_maximum_fusion.weight_ref), custom_call_target="tpu_custom_call" | custom-call | flops 8493465600 | bytes 4000000 | tf_op jit(solution)/shard_map/tower/pallas_call | solution.py:296
  14.2 6.9 %collective-permute-done.4.weight_ref = bf16[2320,128]{1,0:T(8,128)(2,1)} collective-permute-done((bf16[2320,128]{1,0:T(8,128)(2,1)}, bf16[2320,128]{1,0:T(8,128)(2,1)}, u32[]{:S(2)}, u32[]{:S(2)}) %collective-permute-start.4) | collective-permute-done | bytes 593952 | tf_op jit(solution)/shard_map/ppermute | solution.py:357
  21.1 4.8 %tower.9 = (bf16[32,100,128]{2,1,0:T(8,128)(2,1)S(1)}, bf16[32,100,128]{2,1,0:T(8,128)(2,1)S(1)}, bf16[2368,128]{1,0:T(8,128)(2,1)S(1)}) custom-call(s32[9]{0:T(128)S(1)} %get-tuple-element.87.slots_ref, bf16[32,100,128]{2,1,0:T(8,128)(2,1)S(1)} %bitcast.64, bf16[32,100,128]{2,1,0:T(8,128)(2,1)S(1)} %bitcast.72, ...), custom_call_target="tpu_custom_call", output_to_operand_aliasing={{0}: (4, {}), {1}: (5, {})} | custom-call | flops 8493465600 | bytes 4000000 | tf_op jit(solution)/shard_map/tower/pallas_call | solution.py:296
  25.9 0.6 collective-permute-start.14
  26.4 8.7 %collective-permute-done.2.weight_ref = bf16[2320,128]{1,0:T(8,128)(2,1)} collective-permute-done((bf16[2320,128]{1,0:T(8,128)(2,1)}, bf16[2320,128]{1,0:T(8,128)(2,1)}, u32[]{:S(2)}, u32[]{:S(2)}) %collective-permute-start.2) | collective-permute-done | bytes 593952 | tf_op jit(solution)/shard_map/ppermute | solution.py:357
  35.1 0.5 collective-permute-start.1
  35.6 4.6 %tower.10 = (bf16[32,100,128]{2,1,0:T(8,128)(2,1)S(1)}, bf16[32,100,128]{2,1,0:T(8,128)(2,1)S(1)}, bf16[2368,128]{1,0:T(8,128)(2,1)S(1)}) custom-call(s32[9]{0:T(128)S(1)} %get-tuple-element.88.slots_ref, bf16[32,100,128]{2,1,0:T(8,128)(2,1)S(1)} %bitcast.65, bf16[32,100,128]{2,1,0:T(8,128)(2,1)S(1)} %bitcast.73, ...), custom_call_target="tpu_custom_call", output_to_operand_aliasing={{0}: (4, {}), {1}: (5, {})} | custom-call | flops 8493465600 | bytes 4000000 | tf_op jit(solution)/shard_map/tower/pallas_call | solution.py:296
  40.3 4.6 %tower.11 = (bf16[32,100,128]{2,1,0:T(8,128)(2,1)S(1)}, bf16[32,100,128]{2,1,0:T(8,128)(2,1)S(1)}, bf16[2368,128]{1,0:T(8,128)(2,1)S(1)}) custom-call(s32[9]{0:T(128)S(1)} %get-tuple-element.89.slots_ref, bf16[32,100,128]{2,1,0:T(8,128)(2,1)S(1)} %bitcast.66, bf16[32,100,128]{2,1,0:T(8,128)(2,1)S(1)} %bitcast.74, ...), custom_call_target="tpu_custom_call", output_to_operand_aliasing={{0}: (4, {}), {1}: (5, {})} | custom-call | flops 8493465600 | bytes 4000000 | tf_op jit(solution)/shard_map/tower/pallas_call | solution.py:296
  45.0 0.2 add_convert_fusion.1.rest_2_
  45.2 1.3 %collective-permute-start.15 = (bf16[2368,128]{1,0:T(8,128)(2,1)S(1)}, bf16[2368,128]{1,0:T(8,128)(2,1)S(1)}, u32[]{:S(2)}, u32[]{:S(2)}) collective-permute-start(bf16[2368,128]{1,0:T(8,128)(2,1)S(1)} %add_convert_fusion.1.rest_2_), channel_id=1, source_target_pairs={{0,2},{1,3},{2,0},{3,1},{4,6},{5,7},{6,4},{7,5},{8,10},{9,11},{10,... | collective-permute-start | bytes 1818632 | tf_op jit(solution)/shard_map/ppermute | solution.py:357
  46.5 4.9 %tower.12 = (bf16[32,100,128]{2,1,0:T(8,128)(2,1)S(1)}, bf16[32,100,128]{2,1,0:T(8,128)(2,1)S(1)}, bf16[2368,128]{1,0:T(8,128)(2,1)S(1)}) custom-call(s32[9]{0:T(128)S(1)} %get-tuple-element.90.slots_ref, bf16[32,100,128]{2,1,0:T(8,128)(2,1)S(1)} %bitcast.67, bf16[32,100,128]{2,1,0:T(8,128)(2,1)S(1)} %bitcast.75, ...), custom_call_target="tpu_custom_call", output_to_operand_aliasing={{0}: (4, {}), {1}: (5, {})} | custom-call | flops 8493465600 | bytes 4000000 | tf_op jit(solution)/shard_map/tower/pallas_call | solution.py:296
  51.4 4.6 %tower.13 = (bf16[32,100,128]{2,1,0:T(8,128)(2,1)S(1)}, bf16[32,100,128]{2,1,0:T(8,128)(2,1)S(1)}, bf16[2368,128]{1,0:T(8,128)(2,1)S(1)}) custom-call(s32[9]{0:T(128)S(1)} %get-tuple-element.91.slots_ref, bf16[32,100,128]{2,1,0:T(8,128)(2,1)S(1)} %bitcast.68, bf16[32,100,128]{2,1,0:T(8,128)(2,1)S(1)} %bitcast.76, ...), custom_call_target="tpu_custom_call", output_to_operand_aliasing={{0}: (4, {}), {1}: (5, {})} | custom-call | flops 8493465600 | bytes 4000000 | tf_op jit(solution)/shard_map/tower/pallas_call | solution.py:296
  56.1 0.2 add_convert_fusion.rest_2_
  56.2 1.9 %collective-permute-start.16 = (bf16[2368,128]{1,0:T(8,128)(2,1)S(1)}, bf16[2368,128]{1,0:T(8,128)(2,1)S(1)}, u32[]{:S(2)}, u32[]{:S(2)}) collective-permute-start(bf16[2368,128]{1,0:T(8,128)(2,1)S(1)} %add_convert_fusion.rest_2_), channel_id=1, source_target_pairs={{0,4},{1,5},{2,6},{3,7},{4,0},{5,1},{6,2},{7,3},{8,12},{9,13},{10,... | collective-permute-start | bytes 1818632 | tf_op jit(solution)/shard_map/ppermute | solution.py:357
  58.2 4.6 %tower.14 = (bf16[32,100,128]{2,1,0:T(8,128)(2,1)S(1)}, bf16[32,100,128]{2,1,0:T(8,128)(2,1)S(1)}, bf16[2368,128]{1,0:T(8,128)(2,1)S(1)}) custom-call(s32[9]{0:T(128)S(1)} %get-tuple-element.92.slots_ref, bf16[32,100,128]{2,1,0:T(8,128)(2,1)S(1)} %bitcast.69, bf16[32,100,128]{2,1,0:T(8,128)(2,1)S(1)} %bitcast.77, ...), custom_call_target="tpu_custom_call", output_to_operand_aliasing={{0}: (4, {}), {1}: (5, {})} | custom-call | flops 8493465600 | bytes 4000000 | tf_op jit(solution)/shard_map/tower/pallas_call | solution.py:296
  62.8 4.9 %tower.15 = (bf16[32,100,128]{2,1,0:T(8,128)(2,1)S(1)}, bf16[32,100,128]{2,1,0:T(8,128)(2,1)S(1)}, bf16[2368,128]{1,0:T(8,128)(2,1)S(1)}) custom-call(s32[9]{0:T(128)S(1)} %get-tuple-element.93.slots_ref, bf16[32,100,128]{2,1,0:T(8,128)(2,1)S(1)} %bitcast.70, bf16[32,100,128]{2,1,0:T(8,128)(2,1)S(1)} %bitcast.78, ...), custom_call_target="tpu_custom_call", output_to_operand_aliasing={{0}: (4, {}), {1}: (5, {})} | custom-call | flops 8493465600 | bytes 4000000 | tf_op jit(solution)/shard_map/tower/pallas_call | solution.py:296
  67.7 0.1 convert_add_fusion.1
  68.0 1.6 %collective-permute-start.10 = (bf16[592,128]{1,0:T(8,128)(2,1)S(1)}, bf16[592,128]{1,0:T(8,128)(2,1)S(1)}, u32[]{:S(2)}, u32[]{:S(2)}) collective-permute-start(bf16[592,128]{1,0:T(8,128)(2,1)S(1)} %get-tuple-element.80), channel_id=1, source_target_pairs={{0,8},{8,0},{16,24},{24,16},{1,9},{9,1},{17,25},{25,17},{2,10},{10... | collective-permute-start | bytes 454664 | tf_op jit(solution)/shard_map/ppermute | solution.py:357
  69.6 2.6 %collective-permute-start.11 = (bf16[592,128]{1,0:T(8,128)(2,1)S(1)}, bf16[592,128]{1,0:T(8,128)(2,1)S(1)}, u32[]{:S(2)}, u32[]{:S(2)}) collective-permute-start(bf16[592,128]{1,0:T(8,128)(2,1)S(1)} %get-tuple-element.82), channel_id=1, source_target_pairs={{0,16},{8,24},{16,0},{24,8},{1,17},{9,25},{17,1},{25,9},{2,18},{10... | collective-permute-start | bytes 454664 | tf_op jit(solution)/shard_map/ppermute | solution.py:357
  72.2 0.2 collective-permute-start.12
  72.5 0.1 collective-permute-done.16
  72.6 0.3 convert_add_fusion
  73.0 1.7 %collective-permute-start.17 = (bf16[592,128]{1,0:T(8,128)(2,1)S(1)}, bf16[592,128]{1,0:T(8,128)(2,1)S(1)}, u32[]{:S(2)}, u32[]{:S(2)}) collective-permute-start(bf16[592,128]{1,0:T(8,128)(2,1)S(1)} %get-tuple-element.83), channel_id=1, source_target_pairs={{0,8},{8,0},{16,24},{24,16},{1,9},{9,1},{17,25},{25,17},{2,10},{10... | collective-permute-start | bytes 454664 | tf_op jit(solution)/shard_map/ppermute | solution.py:357
  74.7 2.8 %collective-permute-start.18 = (bf16[592,128]{1,0:T(8,128)(2,1)S(1)}, bf16[592,128]{1,0:T(8,128)(2,1)S(1)}, u32[]{:S(2)}, u32[]{:S(2)}) collective-permute-start(bf16[592,128]{1,0:T(8,128)(2,1)S(1)} %get-tuple-element.85), channel_id=1, source_target_pairs={{0,16},{8,24},{16,0},{24,8},{1,17},{9,25},{17,1},{25,9},{2,18},{10... | collective-permute-start | bytes 454664 | tf_op jit(solution)/shard_map/ppermute | solution.py:357
  77.5 2.0 %collective-permute-start.19 = (bf16[592,128]{1,0:T(8,128)(2,1)S(1)}, bf16[592,128]{1,0:T(8,128)(2,1)S(1)}, u32[]{:S(2)}, u32[]{:S(2)}) collective-permute-start(bf16[592,128]{1,0:T(8,128)(2,1)S(1)} %get-tuple-element.84), channel_id=1, source_target_pairs={{0,24},{8,16},{16,8},{24,0},{1,25},{9,17},{17,9},{25,1},{2,26},{10... | collective-permute-start | bytes 454664 | tf_op jit(solution)/shard_map/ppermute | solution.py:357
  79.5 4.4 %collective-permute-done.11 = bf16[592,128]{1,0:T(8,128)(2,1)S(1)} collective-permute-done((bf16[592,128]{1,0:T(8,128)(2,1)S(1)}, bf16[592,128]{1,0:T(8,128)(2,1)S(1)}, u32[]{:S(2)}, u32[]{:S(2)}) %collective-permute-start.11) | collective-permute-done | bytes 151584 | tf_op jit(solution)/shard_map/ppermute | solution.py:357
  84.0 1.2 %collective-permute-start.13 = (bf16[592,128]{1,0:T(8,128)(2,1)S(1)}, bf16[592,128]{1,0:T(8,128)(2,1)S(1)}, u32[]{:S(2)}, u32[]{:S(2)}) collective-permute-start(bf16[592,128]{1,0:T(8,128)(2,1)S(1)} %fusion.6), channel_id=1, source_target_pairs={{0,6},{1,7},{2,4},{3,5},{4,2},{5,3},{6,0},{7,1},{8,14},{9,15},{10,... | collective-permute-start | bytes 454664 | tf_op jit(solution)/shard_map/ppermute | solution.py:357
  85.2 11.7 %collective-permute-done.18 = bf16[592,128]{1,0:T(8,128)(2,1)S(1)} collective-permute-done((bf16[592,128]{1,0:T(8,128)(2,1)S(1)}, bf16[592,128]{1,0:T(8,128)(2,1)S(1)}, u32[]{:S(2)}, u32[]{:S(2)}) %collective-permute-start.18) | collective-permute-done | bytes 151584 | tf_op jit(solution)/shard_map/ppermute | solution.py:357
  97.0 2.5 %collective-permute-start.20 = (bf16[592,128]{1,0:T(8,128)(2,1)S(1)}, bf16[592,128]{1,0:T(8,128)(2,1)S(1)}, u32[]{:S(2)}, u32[]{:S(2)}) collective-permute-start(bf16[592,128]{1,0:T(8,128)(2,1)S(1)} %fusion.3), channel_id=1, source_target_pairs={{0,24},{8,16},{16,8},{24,0},{1,25},{9,17},{17,9},{25,1},{2,26},{10... | collective-permute-start | bytes 454664 | tf_op jit(solution)/shard_map/ppermute | solution.py:357
  99.5 2.6 %collective-permute-start.21 = (bf16[592,128]{1,0:T(8,128)(2,1)S(1)}, bf16[592,128]{1,0:T(8,128)(2,1)S(1)}, u32[]{:S(2)}, u32[]{:S(2)}) collective-permute-start(bf16[592,128]{1,0:T(8,128)(2,1)S(1)} %fusion.3), channel_id=1, source_target_pairs={{0,16},{8,24},{16,0},{24,8},{1,17},{9,25},{17,1},{25,9},{2,18},{10... | collective-permute-start | bytes 454664 | tf_op jit(solution)/shard_map/ppermute | solution.py:357
  102.1 1.5 %copy.49 = bf16[16,2,100,128]{3,1,2,0:T(2,128)(2,1)} copy(bf16[16,2,100,128]{3,2,1,0:T(8,128)(2,1)S(1)} %bitcast.79) | data formatting | bytes 1638400
  103.6 1.5 %copy.50 = bf16[16,2,100,128]{3,1,2,0:T(2,128)(2,1)} copy(bf16[16,2,100,128]{3,2,1,0:T(8,128)(2,1)S(1)} %bitcast.80) | data formatting | bytes 1638400
  105.2 0.3 collective-permute-done.20
  105.5 6.6 %collective-permute-done.21 = bf16[592,128]{1,0:T(8,128)(2,1)S(1)} collective-permute-done((bf16[592,128]{1,0:T(8,128)(2,1)S(1)}, bf16[592,128]{1,0:T(8,128)(2,1)S(1)}, u32[]{:S(2)}, u32[]{:S(2)}) %collective-permute-start.21) | collective-permute-done | bytes 151584 | tf_op jit(solution)/shard_map/ppermute | solution.py:357
  112.1 0.5 convert_add_fusion.2
  112.8 1.1 copy.47
  113.9 1.0 copy.48
  (46 shorter events, 1.3 us)
Async XLA Ops:
  0.6 7.4 %copy-start.2 = (s32[16,2]{0,1:T(2,128)S(1)}, s32[16,2]{0,1:T(2,128)}, u32[]{:S(2)}) copy-start(s32[16,2]{0,1:T(2,128)} %param.9) | copy-start | bytes 388
  0.6 8.2 %copy-start = (bf16[16,2,100,128]{3,1,2,0:T(2,128)(2,1)S(1)}, bf16[16,2,100,128]{3,1,2,0:T(2,128)(2,1)}, u32[]{:S(2)}) copy-start(bf16[16,2,100,128]{3,1,2,0:T(2,128)(2,1)} %param.7) | copy-start | bytes 2457604
  1.6 7.4 %copy-start.1 = (bf16[16,2,100,128]{3,1,2,0:T(2,128)(2,1)S(1)}, bf16[16,2,100,128]{3,1,2,0:T(2,128)(2,1)}, u32[]{:S(2)}) copy-start(bf16[16,2,100,128]{3,1,2,0:T(2,128)(2,1)} %param.8) | copy-start | bytes 2457604
  3.6 17.5 %collective-permute-start.6 = (bf16[2320,128]{1,0:T(8,128)(2,1)}, bf16[2320,128]{1,0:T(8,128)(2,1)}, u32[]{:S(2)}, u32[]{:S(2)}) collective-permute-start(bf16[2320,128]{1,0:T(8,128)(2,1)} %pad_maximum_fusion.weight_ref), channel_id=1, source_target_pairs={{0,1},{1,0},{2,3},{3,2},{4,5},{5,4},{6,7},{7,6},{8,9},{9,8},{10,11... | collective-permute-start | bytes 1781768 | tf_op jit(solution)/shard_map/ppermute | solution.py:357
  4.0 17.1 %collective-permute-start.4 = (bf16[2320,128]{1,0:T(8,128)(2,1)}, bf16[2320,128]{1,0:T(8,128)(2,1)}, u32[]{:S(2)}, u32[]{:S(2)}) collective-permute-start(bf16[2320,128]{1,0:T(8,128)(2,1)} %pad_maximum_fusion.weight_ref), channel_id=1, source_target_pairs={{0,2},{1,3},{2,0},{3,1},{4,6},{5,7},{6,4},{7,5},{8,10},{9,11},{10,... | collective-permute-start | bytes 1781768 | tf_op jit(solution)/shard_map/ppermute | solution.py:357
  6.5 28.6 %collective-permute-start.2 = (bf16[2320,128]{1,0:T(8,128)(2,1)}, bf16[2320,128]{1,0:T(8,128)(2,1)}, u32[]{:S(2)}, u32[]{:S(2)}) collective-permute-start(bf16[2320,128]{1,0:T(8,128)(2,1)} %pad_maximum_fusion.weight_ref), channel_id=1, source_target_pairs={{0,4},{1,5},{2,6},{3,7},{4,0},{5,1},{6,2},{7,3},{8,12},{9,13},{10,... | collective-permute-start | bytes 1781768 | tf_op jit(solution)/shard_map/ppermute | solution.py:357
  8.0 27.1 %collective-permute-start = (bf16[2320,128]{1,0:T(8,128)(2,1)}, bf16[2320,128]{1,0:T(8,128)(2,1)}, u32[]{:S(2)}, u32[]{:S(2)}) collective-permute-start(bf16[2320,128]{1,0:T(8,128)(2,1)} %pad_maximum_fusion.weight_ref), channel_id=1, source_target_pairs={{0,6},{1,7},{2,4},{3,5},{4,2},{5,3},{6,0},{7,1},{8,14},{9,15},{10,... | collective-permute-start | bytes 1781768 | tf_op jit(solution)/shard_map/ppermute | solution.py:357
  21.1 14.5 %collective-permute-start.5 = (bf16[2320,128]{1,0:T(8,128)(2,1)}, bf16[2320,128]{1,0:T(8,128)(2,1)S(1)}, u32[]{:S(2)}, u32[]{:S(2)}) collective-permute-start(bf16[2320,128]{1,0:T(8,128)(2,1)} %collective-permute-done.4.weight_ref), channel_id=1, source_target_pairs={{0,1},{1,0},{2,3},{3,2},{4,5},{5,4},{6,7},{7,6},{8,9},{9,8},{10,11... | collective-permute-start | bytes 1781768 | tf_op jit(solution)/shard_map/ppermute | solution.py:357
  25.9 46.4 %collective-permute-start.14 = (bf16[2368,128]{1,0:T(8,128)(2,1)S(1)}, bf16[2368,128]{1,0:T(8,128)(2,1)S(1)}, u32[]{:S(2)}, u32[]{:S(2)}) collective-permute-start(bf16[2368,128]{1,0:T(8,128)(2,1)S(1)} %get-tuple-element.53), channel_id=1, source_target_pairs={{0,1},{1,0},{2,3},{3,2},{4,5},{5,4},{6,7},{7,6},{8,9},{9,8},{10,11... | collective-permute-start | bytes 1818632 | tf_op jit(solution)/shard_map/ppermute | solution.py:357
  35.1 11.4 %collective-permute-start.3 = (bf16[2320,128]{1,0:T(8,128)(2,1)}, bf16[2320,128]{1,0:T(8,128)(2,1)S(1)}, u32[]{:S(2)}, u32[]{:S(2)}) collective-permute-start(bf16[2320,128]{1,0:T(8,128)(2,1)} %collective-permute-done.2.weight_ref), channel_id=1, source_target_pairs={{0,1},{1,0},{2,3},{3,2},{4,5},{5,4},{6,7},{7,6},{8,9},{9,8},{10,11... | collective-permute-start | bytes 1781768 | tf_op jit(solution)/shard_map/ppermute | solution.py:357
  35.1 23.1 %collective-permute-start.1 = (bf16[2320,128]{1,0:T(8,128)(2,1)}, bf16[2320,128]{1,0:T(8,128)(2,1)S(1)}, u32[]{:S(2)}, u32[]{:S(2)}) collective-permute-start(bf16[2320,128]{1,0:T(8,128)(2,1)} %collective-permute-done.weight_ref), channel_id=1, source_target_pairs={{0,1},{1,0},{2,3},{3,2},{4,5},{5,4},{6,7},{7,6},{8,9},{9,8},{10,11... | collective-permute-start | bytes 1781768 | tf_op jit(solution)/shard_map/ppermute | solution.py:357
  40.3 4.7 %collective-permute-start.7 = (bf16[2368,128]{1,0:T(8,128)(2,1)S(1)}, bf16[2368,128]{1,0:T(8,128)(2,1)S(1)}, u32[]{:S(2)}, u32[]{:S(2)}) collective-permute-start(bf16[2368,128]{1,0:T(8,128)(2,1)S(1)} %get-tuple-element.39), channel_id=1, source_target_pairs={{0,1},{1,0},{2,3},{3,2},{4,5},{5,4},{6,7},{7,6},{8,9},{9,8},{10,11... | collective-permute-start | bytes 1818632 | tf_op jit(solution)/shard_map/ppermute | solution.py:357
  45.2 27.3 %collective-permute-start.15 = (bf16[2368,128]{1,0:T(8,128)(2,1)S(1)}, bf16[2368,128]{1,0:T(8,128)(2,1)S(1)}, u32[]{:S(2)}, u32[]{:S(2)}) collective-permute-start(bf16[2368,128]{1,0:T(8,128)(2,1)S(1)} %add_convert_fusion.1.rest_2_), channel_id=1, source_target_pairs={{0,2},{1,3},{2,0},{3,1},{4,6},{5,7},{6,4},{7,5},{8,10},{9,11},{10,... | collective-permute-start | bytes 1818632 | tf_op jit(solution)/shard_map/ppermute | solution.py:357
  51.3 4.7 %collective-permute-start.8 = (bf16[2368,128]{1,0:T(8,128)(2,1)S(1)}, bf16[2368,128]{1,0:T(8,128)(2,1)S(1)}, u32[]{:S(2)}, u32[]{:S(2)}) collective-permute-start(bf16[2368,128]{1,0:T(8,128)(2,1)S(1)} %get-tuple-element.45), channel_id=1, source_target_pairs={{0,1},{1,0},{2,3},{3,2},{4,5},{5,4},{6,7},{7,6},{8,9},{9,8},{10,11... | collective-permute-start | bytes 1818632 | tf_op jit(solution)/shard_map/ppermute | solution.py:357
  56.2 16.4 %collective-permute-start.16 = (bf16[2368,128]{1,0:T(8,128)(2,1)S(1)}, bf16[2368,128]{1,0:T(8,128)(2,1)S(1)}, u32[]{:S(2)}, u32[]{:S(2)}) collective-permute-start(bf16[2368,128]{1,0:T(8,128)(2,1)S(1)} %add_convert_fusion.rest_2_), channel_id=1, source_target_pairs={{0,4},{1,5},{2,6},{3,7},{4,0},{5,1},{6,2},{7,3},{8,12},{9,13},{10,... | collective-permute-start | bytes 1818632 | tf_op jit(solution)/shard_map/ppermute | solution.py:357
  62.8 5.0 %collective-permute-start.9 = (bf16[2368,128]{1,0:T(8,128)(2,1)S(1)}, bf16[2368,128]{1,0:T(8,128)(2,1)S(1)}, u32[]{:S(2)}, u32[]{:S(2)}) collective-permute-start(bf16[2368,128]{1,0:T(8,128)(2,1)S(1)} %get-tuple-element.51), channel_id=1, source_target_pairs={{0,1},{1,0},{2,3},{3,2},{4,5},{5,4},{6,7},{7,6},{8,9},{9,8},{10,11... | collective-permute-start | bytes 1818632 | tf_op jit(solution)/shard_map/ppermute | solution.py:357
  68.0 9.5 %collective-permute-start.10 = (bf16[592,128]{1,0:T(8,128)(2,1)S(1)}, bf16[592,128]{1,0:T(8,128)(2,1)S(1)}, u32[]{:S(2)}, u32[]{:S(2)}) collective-permute-start(bf16[592,128]{1,0:T(8,128)(2,1)S(1)} %get-tuple-element.80), channel_id=1, source_target_pairs={{0,8},{8,0},{16,24},{24,16},{1,9},{9,1},{17,25},{25,17},{2,10},{10... | collective-permute-start | bytes 454664 | tf_op jit(solution)/shard_map/ppermute | solution.py:357
  69.6 14.3 %collective-permute-start.11 = (bf16[592,128]{1,0:T(8,128)(2,1)S(1)}, bf16[592,128]{1,0:T(8,128)(2,1)S(1)}, u32[]{:S(2)}, u32[]{:S(2)}) collective-permute-start(bf16[592,128]{1,0:T(8,128)(2,1)S(1)} %get-tuple-element.82), channel_id=1, source_target_pairs={{0,16},{8,24},{16,0},{24,8},{1,17},{9,25},{17,1},{25,9},{2,18},{10... | collective-permute-start | bytes 454664 | tf_op jit(solution)/shard_map/ppermute | solution.py:357
  72.2 11.7 %collective-permute-start.12 = (bf16[592,128]{1,0:T(8,128)(2,1)S(1)}, bf16[592,128]{1,0:T(8,128)(2,1)S(1)}, u32[]{:S(2)}, u32[]{:S(2)}) collective-permute-start(bf16[592,128]{1,0:T(8,128)(2,1)S(1)} %get-tuple-element.81), channel_id=1, source_target_pairs={{0,24},{8,16},{16,8},{24,0},{1,25},{9,17},{17,9},{25,1},{2,26},{10... | collective-permute-start | bytes 454664 | tf_op jit(solution)/shard_map/ppermute | solution.py:357
  73.0 12.2 %collective-permute-start.17 = (bf16[592,128]{1,0:T(8,128)(2,1)S(1)}, bf16[592,128]{1,0:T(8,128)(2,1)S(1)}, u32[]{:S(2)}, u32[]{:S(2)}) collective-permute-start(bf16[592,128]{1,0:T(8,128)(2,1)S(1)} %get-tuple-element.83), channel_id=1, source_target_pairs={{0,8},{8,0},{16,24},{24,16},{1,9},{9,1},{17,25},{25,17},{2,10},{10... | collective-permute-start | bytes 454664 | tf_op jit(solution)/shard_map/ppermute | solution.py:357
  74.7 22.2 %collective-permute-start.18 = (bf16[592,128]{1,0:T(8,128)(2,1)S(1)}, bf16[592,128]{1,0:T(8,128)(2,1)S(1)}, u32[]{:S(2)}, u32[]{:S(2)}) collective-permute-start(bf16[592,128]{1,0:T(8,128)(2,1)S(1)} %get-tuple-element.85), channel_id=1, source_target_pairs={{0,16},{8,24},{16,0},{24,8},{1,17},{9,25},{17,1},{25,9},{2,18},{10... | collective-permute-start | bytes 454664 | tf_op jit(solution)/shard_map/ppermute | solution.py:357
  77.5 19.4 %collective-permute-start.19 = (bf16[592,128]{1,0:T(8,128)(2,1)S(1)}, bf16[592,128]{1,0:T(8,128)(2,1)S(1)}, u32[]{:S(2)}, u32[]{:S(2)}) collective-permute-start(bf16[592,128]{1,0:T(8,128)(2,1)S(1)} %get-tuple-element.84), channel_id=1, source_target_pairs={{0,24},{8,16},{16,8},{24,0},{1,25},{9,17},{17,9},{25,1},{2,26},{10... | collective-permute-start | bytes 454664 | tf_op jit(solution)/shard_map/ppermute | solution.py:357
  84.0 12.9 %collective-permute-start.13 = (bf16[592,128]{1,0:T(8,128)(2,1)S(1)}, bf16[592,128]{1,0:T(8,128)(2,1)S(1)}, u32[]{:S(2)}, u32[]{:S(2)}) collective-permute-start(bf16[592,128]{1,0:T(8,128)(2,1)S(1)} %fusion.6), channel_id=1, source_target_pairs={{0,6},{1,7},{2,4},{3,5},{4,2},{5,3},{6,0},{7,1},{8,14},{9,15},{10,... | collective-permute-start | bytes 454664 | tf_op jit(solution)/shard_map/ppermute | solution.py:357
  97.0 8.5 %collective-permute-start.20 = (bf16[592,128]{1,0:T(8,128)(2,1)S(1)}, bf16[592,128]{1,0:T(8,128)(2,1)S(1)}, u32[]{:S(2)}, u32[]{:S(2)}) collective-permute-start(bf16[592,128]{1,0:T(8,128)(2,1)S(1)} %fusion.3), channel_id=1, source_target_pairs={{0,24},{8,16},{16,8},{24,0},{1,25},{9,17},{17,9},{25,1},{2,26},{10... | collective-permute-start | bytes 454664 | tf_op jit(solution)/shard_map/ppermute | solution.py:357
  99.5 12.6 %collective-permute-start.21 = (bf16[592,128]{1,0:T(8,128)(2,1)S(1)}, bf16[592,128]{1,0:T(8,128)(2,1)S(1)}, u32[]{:S(2)}, u32[]{:S(2)}) collective-permute-start(bf16[592,128]{1,0:T(8,128)(2,1)S(1)} %fusion.3), channel_id=1, source_target_pairs={{0,16},{8,24},{16,0},{24,8},{1,17},{9,25},{17,1},{25,9},{2,18},{10... | collective-permute-start | bytes 454664 | tf_op jit(solution)/shard_map/ppermute | solution.py:357
  102.1 10.0 %collective-permute-start.22 = (bf16[592,128]{1,0:T(8,128)(2,1)S(1)}, bf16[592,128]{1,0:T(8,128)(2,1)S(1)}, u32[]{:S(2)}, u32[]{:S(2)}) collective-permute-start(bf16[592,128]{1,0:T(8,128)(2,1)S(1)} %fusion.3), channel_id=1, source_target_pairs={{0,8},{8,0},{16,24},{24,16},{1,9},{9,1},{17,25},{25,17},{2,10},{10... | collective-permute-start | bytes 454664 | tf_op jit(solution)/shard_map/ppermute | solution.py:357
